TPU v7x, 512 devices: a whole 4x4x16 slice. The times are simulated.
512 devices in a mesh: gx: 8 (over y, core), gy: 4 (over z_hi), gz: 16 (over z_lo, x).
Axes of the slice: x: 4, y: 4, z: 16 (z_hi: 4, z_lo: 4; z = z_hi * 4 + z_lo), core: 2. Of those that a mesh axis runs over, the one named last changes fastest.
Arguments:
- blocks: float32 [8, 4, 16, 8, 128, 128], P('gx', 'gy', 'gz'), as said below
- columns: int32 [8, 4, 16, 8], replicated, may hold values from -1 to 511, as said below
Outputs:
- purified: float32 [8, 4, 16, 8, 128, 128], P('gx', 'gy', 'gz')
Inputs may be any that keep to these rules, and one draw needn't show every extreme that they name: columns[i, 0] is i itself; every other entry is -1 or the number of a cluster that differs from i by one along exactly one of the three dimensions, repeats allowed. `blocks`: a block in a slot whose column is -1 is zero.
All inputs are finite; a program needn't handle non-finite values.
Results may differ from a plain program's by a relative error of at most 0.0003.
Values sent between devices are 32-bit elements; how exact they have to be, the bound alone decides.
No kernel may reach another device: no remote copies, remote signals or barrier semaphores. Data moves between devices by JAX's collectives and lax.ppermute only.
A program may use at most 64 MiB of HBM per device.

v0:
```python
import jax
import jax.numpy as jnp
from jax import lax
from jax.sharding import PartitionSpec as P

exact_mode = lax.Precision.HIGHEST


def with_halo(cells, sides, width):
    for axis, dim in sides:
        count = lax.axis_size(axis)
        ends = count - 1
        head = lax.slice_in_dim(cells, 0, width, axis=dim)
        tail = lax.slice_in_dim(cells, cells.shape[dim] - width, cells.shape[dim], axis=dim)
        cells = jnp.concatenate(
            [
                lax.ppermute(tail, axis, [(i, (i + 1) % count) for i in range(ends)]),
                cells,
                lax.ppermute(head, axis, [((i + 1) % count, i) for i in range(ends)]),
            ],
            axis=dim,
        )
    return cells


def extend(current):
    padded = with_halo(current, (("gx", 0), ("gy", 1), ("gz", 2)), 1)
    return padded


def purify(current, slot_index, matches):
    kslots, block_size = (current.shape[3], current.shape[4])
    padded = extend(current).reshape(-1, kslots, block_size, block_size)
    flat_current = current.reshape(-1, kslots, block_size, block_size)
    far_rows = padded[slot_index[0]]
    picked = jnp.einsum("tus,tuab->tsab", matches[0], far_rows, precision=exact_mode)
    row_blocks = flat_current[0]
    square = jnp.einsum("tab,tsbc->sac", row_blocks, picked, precision=exact_mode)
    cubed = jnp.einsum("tab,tsbc->sac", square, picked, precision=exact_mode)
    renewed = 3.0 * square - 2.0 * cubed
    results = [renewed]
    return jnp.stack(results).reshape(current.shape)


def on_device(blocks, columns):
    span_x, span_y, span_z, kslots = (
        blocks.shape[0],
        blocks.shape[1],
        blocks.shape[2],
        blocks.shape[3],
    )
    total_y, total_z = (columns.shape[1], columns.shape[2])
    flat_cols = columns.reshape(-1, kslots)
    base_x = lax.axis_index("gx") * span_x
    base_y = lax.axis_index("gy") * span_y
    base_z = lax.axis_index("gz") * span_z
    own_cols = lax.dynamic_slice(
        columns, (base_x, base_y, base_z, jnp.int32(0)), (span_x, span_y, span_z, kslots)
    ).reshape(-1, kslots)
    safe_cols = jnp.maximum(own_cols, 0)
    pos_x = jnp.clip(safe_cols // (total_y * total_z) - base_x + 1, 0, span_x + 1)
    pos_y = jnp.clip(safe_cols // total_z % total_y - base_y + 1, 0, span_y + 1)
    pos_z = jnp.clip(safe_cols % total_z - base_z + 1, 0, span_z + 1)
    slot_index = (pos_x * (span_y + 2) + pos_y) * (span_z + 2) + pos_z
    far_cols = flat_cols[safe_cols]
    target = own_cols[:, None, None, :]
    matches = (
        (far_cols[:, :, :, None] == target) & (target >= 0) & (own_cols[:, :, None, None] >= 0)
    )
    matches = matches.astype(jnp.float32)
    current = blocks
    current = purify(current, slot_index, matches)
    return current


def solution(mesh):
    return jax.shard_map(
        on_device,
        mesh=mesh,
        in_specs=(P("gx", "gy", "gz", None, None, None), P()),
        out_specs=P("gx", "gy", "gz", None, None, None),
        check_vma=False,
    )
```

profile of v0, /device:TPU:432, one launch (start us, length us, event | category | flops | bytes accessed | tf_op | source)
XLA Modules:
  0.0 318.1 jit_solution(12065977082592249469)
XLA Ops:
  0.0 1.9 collective-permute-start
  1.9 3.6 %collective-permute-start.1 = (f32[1,1,1,8,128,128]{5,4,3,2,1,0:T(8,128)}, f32[1,1,1,8,128,128]{5,4,3,2,1,0:T(8,128)S(1)}, u32[]{:S(2)}, u32[]{:S(2)}) collective-permute-start(f32[1,1,1,8,128,128]{5,4,3,2,1,0:T(8,128)} %param.2), channel_id=1, source_target_pairs={{64,0},{128,64},{192,128},{256,192},{320,256},{384,320},{448,384},... | collective-permute-start | bytes 1572872 | tf_op jit(solution)/shard_map/ppermute | solution.py:19
  5.6 5.1 %collective-permute-done = f32[1,1,1,8,128,128]{5,4,3,2,1,0:T(8,128)S(1)} collective-permute-done((f32[1,1,1,8,128,128]{5,4,3,2,1,0:T(8,128)}, f32[1,1,1,8,128,128]{5,4,3,2,1,0:T(8,128)S(1)}, u32[]{:S(2)}, u32[]{:S(2)}) %collective-permute-start) | collective-permute-done | bytes 524320 | tf_op jit(solution)/shard_map/ppermute | solution.py:17
  10.7 1.1 constant_dynamic-update-slice_fusion.1
  11.8 0.7 collective-permute-done.1
  12.6 0.0 copy-start.3
  12.6 5.7 %collective-permute-start.3 = (f32[3,1,1,8,128,128]{5,4,3,2,1,0:T(8,128)S(1)}, f32[3,1,1,8,128,128]{5,4,3,2,1,0:T(8,128)S(1)}, u32[]{:S(2)}, u32[]{:S(2)}) collective-permute-start(f32[3,1,1,8,128,128]{5,4,3,2,1,0:T(8,128)S(1)} %constant_dynamic-update-slice_fusion), channel_id=1, source_target_pairs={{16,0},{32,16},{48,32},{17,1},{33,17},{49,33},{18,2},{34,18},{50,3... | collective-permute-start | bytes 4718600 | tf_op jit(solution)/shard_map/ppermute | solution.py:19
  18.3 1.3 collective-permute-start.2
  19.6 100.4 %collective-permute-done.3 = f32[3,1,1,8,128,128]{5,4,3,2,1,0:T(8,128)S(1)} collective-permute-done((f32[3,1,1,8,128,128]{5,4,3,2,1,0:T(8,128)S(1)}, f32[3,1,1,8,128,128]{5,4,3,2,1,0:T(8,128)S(1)}, u32[]{:S(2)}, u32[]{:S(2)}) %collective-permute-start.3) | collective-permute-done | bytes 1572896 | tf_op jit(solution)/shard_map/ppermute | solution.py:19
  120.0 0.0 collective-permute-done.2
  120.0 0.0 copy-start.1
  120.0 2.6 pad_maximum_fusion.1
  122.6 0.0 copy-done.1
  122.6 46.6 %collective-permute-start.5 = (f32[3,3,1,8,128,128]{5,4,3,2,1,0:T(8,128)}, f32[3,3,1,8,128,128]{5,4,3,2,1,0:T(8,128)}, u32[]{:S(2)}, u32[]{:S(2)}) collective-permute-start(f32[3,3,1,8,128,128]{5,4,3,2,1,0:T(8,128)} %pad_maximum_fusion.1), channel_id=1, source_target_pairs={{1,0},{2,1},{3,2},{4,3},{5,4},{6,5},{7,6},{8,7},{9,8},{10,9},{11,1... | collective-permute-start | bytes 14155784 | tf_op jit(solution)/shard_map/ppermute | solution.py:19
  169.3 1.9 collective-permute-start.4
  171.2 0.0 copy-done.3
  171.2 0.1 copy.8
  171.4 0.2 compare_reduce_fusion
  171.6 0.2 fusion.31
  171.8 0.6 gather_fusion
  172.4 98.5 %collective-permute-done.5 = f32[3,3,1,8,128,128]{5,4,3,2,1,0:T(8,128)} collective-permute-done((f32[3,3,1,8,128,128]{5,4,3,2,1,0:T(8,128)}, f32[3,3,1,8,128,128]{5,4,3,2,1,0:T(8,128)}, u32[]{:S(2)}, u32[]{:S(2)}) %collective-permute-start.5) | collective-permute-done | bytes 4718624 | tf_op jit(solution)/shard_map/ppermute | solution.py:19
  270.9 6.2 %collective-permute-done.4 = f32[3,3,1,8,128,128]{5,4,3,2,1,0:T(8,128)} collective-permute-done((f32[3,3,1,8,128,128]{5,4,3,2,1,0:T(8,128)}, f32[3,3,1,8,128,128]{5,4,3,2,1,0:T(8,128)}, u32[]{:S(2)}, u32[]{:S(2)}) %collective-permute-start.4) | collective-permute-done | bytes 4718624 | tf_op jit(solution)/shard_map/ppermute | solution.py:17
  277.1 9.6 %pad_maximum_fusion = f32[3,3,3,8,128,128]{5,4,3,2,1,0:T(8,128)} fusion(f32[3,3,1,8,128,128]{5,4,3,2,1,0:T(8,128)} %collective-permute-done.5, f32[3,1,1,8,128,128]{5,4,3,2,1,0:T(8,128)S(1)} %collective-permute-done.3, f32[3,1,1,8,128,128]{5,4,3,2,1,0:T(8,128)S(1)} %constant_dynamic-update-slice_fusion, f32[3,1,1,8,128,128]{5,4,3,2,1,0:T(8,128)} %copy-done.1, ...), kind=kLoop, calls=%fused_computation.2 | loop fusion | flops 14155776 | bytes 28311552 | tf_op jit(solution)/shard_map/concatenate | solution.py:15
  286.7 7.8 %gather_fusion.1 = f32[8,8,128,128]{3,2,1,0:T(8,128)} fusion(f32[27,8,128,128]{3,2,1,0:T(8,128)} %bitcast.84, s32[1024]{0:T(1024)S(1)} %get-tuple-element.14), kind=kCustom, calls=%fused_computation.1 | custom fusion | bytes 8388640 | tf_op jit(solution)/shard_map/gather | solution.py:35
  294.5 8.3 %fusion = f32[8,8,128,128]{3,1,2,0:T(8,128)} fusion(f32[8,8,128,128]{3,2,1,0:T(8,128)} %gather_fusion.1, s32[8,8]{1,0:T(8,128)S(1)} %gather_fusion, s32[8]{0:T(128)S(1)} %get-tuple-element.8, pred[8]{0:T(512)(128)(4,1)S(1)} %broadcast_compare_fusion, pred[8]{0:T(512)(128)(4,1)S(1)} %get-tuple-element.5), kind=kOutput, calls=%fused_computation.4 | convolution fusion | flops 100664832 | bytes 8388912 | tf_op jit(solution)/shard_map/tus,tuab->tsab/dot_general | solution.py:36
  302.8 0.0 copy-start.2
  302.8 5.5 %copy.10 = f32[8,8,128,128]{2,3,0,1:T(8,128)} copy(f32[8,8,128,128]{3,1,2,0:T(8,128)} %fusion) | data formatting | bytes 8388608 | tf_op jit(solution)/shard_map/tus,tuab->tsab/dot_general | solution.py:36
  308.2 0.0 copy-done.2
  308.2 5.4 %fusion.7 = f32[8,128,128,1]{2,1,3,0:T(8,128)S(1)} fusion(f32[8,8,128,128]{2,3,0,1:T(8,128)} %copy.10, f32[1,1,1,8,128,128]{5,4,3,2,1,0:T(8,128)S(1)} %copy-done.2), kind=kOutput, calls=%fused_computation.12 | convolution fusion | flops 1610612736 | bytes 5242880 | tf_op jit(solution)/shard_map/tab,tsbc->sac/dot_general | solution.py:38
  313.6 0.0 copy-done
  313.6 3.4 %fusion.5 = f32[1,1,1,8,128,128]{4,5,3,2,1,0:T(8,128)S(1)} fusion(f32[8,8,128,128]{2,3,0,1:T(8,128)S(1)} %copy-done, f32[8,128,128,1]{2,1,3,0:T(8,128)S(1)} %fusion.7), kind=kOutput, calls=%fused_computation.10 | convolution fusion | flops 1611005952 | bytes 5242880 | tf_op jit(solution)/shard_map/tab,tsbc->sac/dot_general | solution.py:39
  317.1 1.0 copy.13
  (6 shorter events, 0.1 us)
Async XLA Ops:
  0.0 10.7 %collective-permute-start = (f32[1,1,1,8,128,128]{5,4,3,2,1,0:T(8,128)}, f32[1,1,1,8,128,128]{5,4,3,2,1,0:T(8,128)S(1)}, u32[]{:S(2)}, u32[]{:S(2)}) collective-permute-start(f32[1,1,1,8,128,128]{5,4,3,2,1,0:T(8,128)} %param.2), channel_id=1, source_target_pairs={{0,64},{64,128},{128,192},{192,256},{256,320},{320,384},{384,448},... | collective-permute-start | bytes 1572872 | tf_op jit(solution)/shard_map/ppermute | solution.py:17
  1.9 10.6 %collective-permute-start.1 = (f32[1,1,1,8,128,128]{5,4,3,2,1,0:T(8,128)}, f32[1,1,1,8,128,128]{5,4,3,2,1,0:T(8,128)S(1)}, u32[]{:S(2)}, u32[]{:S(2)}) collective-permute-start(f32[1,1,1,8,128,128]{5,4,3,2,1,0:T(8,128)} %param.2), channel_id=1, source_target_pairs={{64,0},{128,64},{192,128},{256,192},{320,256},{384,320},{448,384},... | collective-permute-start | bytes 1572872 | tf_op jit(solution)/shard_map/ppermute | solution.py:19
  12.6 158.6 %copy-start.3 = (s32[8,4,16,8]{2,3,1,0:T(8,128)S(1)}, s32[8,4,16,8]{2,3,1,0:T(8,128)}, u32[]{:S(2)}) copy-start(s32[8,4,16,8]{2,3,1,0:T(8,128)} %param.3) | copy-start | bytes 49156
  12.6 107.4 %collective-permute-start.3 = (f32[3,1,1,8,128,128]{5,4,3,2,1,0:T(8,128)S(1)}, f32[3,1,1,8,128,128]{5,4,3,2,1,0:T(8,128)S(1)}, u32[]{:S(2)}, u32[]{:S(2)}) collective-permute-start(f32[3,1,1,8,128,128]{5,4,3,2,1,0:T(8,128)S(1)} %constant_dynamic-update-slice_fusion), channel_id=1, source_target_pairs={{16,0},{32,16},{48,32},{17,1},{33,17},{49,33},{18,2},{34,18},{50,3... | collective-permute-start | bytes 4718600 | tf_op jit(solution)/shard_map/ppermute | solution.py:19
  18.3 101.7 %collective-permute-start.2 = (f32[3,1,1,8,128,128]{5,4,3,2,1,0:T(8,128)S(1)}, f32[3,1,1,8,128,128]{5,4,3,2,1,0:T(8,128)S(1)}, u32[]{:S(2)}, u32[]{:S(2)}) collective-permute-start(f32[3,1,1,8,128,128]{5,4,3,2,1,0:T(8,128)S(1)} %constant_dynamic-update-slice_fusion), channel_id=1, source_target_pairs={{0,16},{16,32},{32,48},{1,17},{17,33},{33,49},{2,18},{18,34},{34,5... | collective-permute-start | bytes 4718600 | tf_op jit(solution)/shard_map/ppermute | solution.py:17
  120.0 2.6 copy-start.1
  122.6 148.2 %collective-permute-start.5 = (f32[3,3,1,8,128,128]{5,4,3,2,1,0:T(8,128)}, f32[3,3,1,8,128,128]{5,4,3,2,1,0:T(8,128)}, u32[]{:S(2)}, u32[]{:S(2)}) collective-permute-start(f32[3,3,1,8,128,128]{5,4,3,2,1,0:T(8,128)} %pad_maximum_fusion.1), channel_id=1, source_target_pairs={{1,0},{2,1},{3,2},{4,3},{5,4},{6,5},{7,6},{8,7},{9,8},{10,9},{11,1... | collective-permute-start | bytes 14155784 | tf_op jit(solution)/shard_map/ppermute | solution.py:19
  169.3 107.8 %collective-permute-start.4 = (f32[3,3,1,8,128,128]{5,4,3,2,1,0:T(8,128)}, f32[3,3,1,8,128,128]{5,4,3,2,1,0:T(8,128)}, u32[]{:S(2)}, u32[]{:S(2)}) collective-permute-start(f32[3,3,1,8,128,128]{5,4,3,2,1,0:T(8,128)} %pad_maximum_fusion.1), channel_id=1, source_target_pairs={{0,1},{1,2},{2,3},{3,4},{4,5},{5,6},{6,7},{7,8},{8,9},{9,10},{10,1... | collective-permute-start | bytes 14155784 | tf_op jit(solution)/shard_map/ppermute | solution.py:17
  302.8 5.5 %copy-start.2 = (f32[1,1,1,8,128,128]{5,4,3,2,1,0:T(8,128)S(1)}, f32[1,1,1,8,128,128]{5,4,3,2,1,0:T(8,128)}, u32[]{:S(2)}) copy-start(f32[1,1,1,8,128,128]{5,4,3,2,1,0:T(8,128)} %param.2) | copy-start | bytes 1572868
  308.2 5.4 %copy-start = (f32[8,8,128,128]{2,3,0,1:T(8,128)S(1)}, f32[8,8,128,128]{2,3,0,1:T(8,128)}, u32[]{:S(2)}) copy-start(f32[8,8,128,128]{2,3,0,1:T(8,128)} %copy.10) | copy-start | bytes 12582916
where the time goes:
time: 319 us; the launch traced here: 318 us
  waiting for transfers between devices  211 us (66%)
  starting transfers between devices  61.1 us (19%)
  matrix products  17.1 us (5%)
  local copies, waits for them, and re-layouts  16.1 us (5%)
  other arithmetic  12.6 us (4%)
    ppermute x3, waiting for transfers between devices, with_halo(): lax.ppermute(head, axis, [((i + 1) % count, i) for i in range(ends)])  200 us
    ppermute x3, starting transfers between devices, with_halo(): lax.ppermute(head, axis, [((i + 1) % count, i) for i in range(ends)])  56 us
    concatenate x2, other arithmetic, with_halo(): jnp.concatenate([lax.ppermute(tail, axis, [(i, (i + 1) % count) for i in...  12.2 us
    ppermute x3, waiting for transfers between devices, with_halo(): lax.ppermute(tail, axis, [(i, (i + 1) % count) for i in range(ends)])  11.4 us
    dot_general x1, matrix products, purify(): jnp.einsum('tus,tuab->tsab', matches[0], far_rows, precision=exact_mode)  8.32 us
    gather x1, local copies, waits for them, and re-layouts, purify(): far_rows = padded[slot_index[0]]  7.78 us
  transfers between devices with their start and end apart: 6, of which 5 were waited for; matrix products, arithmetic and copies ran while one was open for 1% of the time, Pallas kernels for 0%

commit v1 on v0

v1 whole, which is shorter than its diff:
```python
import functools

import jax
import jax.numpy as jnp
from jax import lax
from jax.experimental import pallas as pl
from jax.experimental.pallas import tpu as pltpu
from jax.sharding import PartitionSpec as P

SIDES = (("gy", 1), ("gy", -1), ("gx", 1), ("gx", -1), ("gz", 1), ("gz", -1))


VMEM_BYTES = 8 * 1024 * 1024


def place(columns_shape):
    _, total_y, _, total_z = columns_shape
    x, y, z = lax.axis_index("gx"), lax.axis_index("gy"), lax.axis_index("gz")
    return (x * total_y + y) * total_z + z, x, y, z


def strides(columns_shape):
    _, total_y, _, total_z = columns_shape
    size = {"gx": total_y * total_z, "gy": total_z, "gz": 1}
    return tuple(step * size[axis] for axis, step in SIDES)


def outgoing(steps, columns, blocks, *rest):
    sends, (rows, sem) = rest[: len(steps)], rest[len(steps) :]
    me, x, y, z = place(columns.shape)
    fetch = pltpu.make_async_copy(columns.at[x, y], rows, sem)
    fetch.start()
    fetch.wait()
    kslots, size = blocks.shape[3], blocks.shape[4]
    weights = []
    for step in steps:
        column = me + step
        weights.append(
            [jnp.where(rows[s, z] == column, 1.0, 0.0).astype(jnp.float32) for s in range(1, kslots)]
        )
    for start in range(0, size, 8):
        part = pl.ds(start, 8)
        own = blocks[0, 0, 0, 0, part, :]
        others = [blocks[0, 0, 0, s, part, :] for s in range(1, kslots)]
        for send, weight in zip(sends, weights):
            send[0, part, :] = own
            send[1, part, :] = sum(w * v for w, v in zip(weight, others))


def halves(value):
    high = value.astype(jnp.bfloat16)
    return high, (value - high.astype(jnp.float32)).astype(jnp.bfloat16)


def left(value):
    high, low = halves(value)
    return jnp.concatenate([high, low, high], axis=1)


def right(value):
    high, low = halves(value)
    return jnp.concatenate([high, high, low], axis=0)


def dot(a, b):
    return jnp.dot(a, b, preferred_element_type=jnp.float32)


def finish(steps, columns, *rest):
    count = len(steps)
    sends, gets = rest[:count], rest[count : 2 * count]
    out, results, rows, sem, out_sems = rest[2 * count :]
    me, x, y, z = place(columns.shape)
    fetch = pltpu.make_async_copy(columns.at[x, y], rows, sem)
    fetch.start()
    fetch.wait()
    kslots, size = out.shape[3], out.shape[4]
    named = [rows[s, z] for s in range(kslots)]
    own = sends[0][0]
    row = jnp.concatenate([own] + [send[1] for send in sends], axis=1)
    row = right(row)
    first = dot(left(own), row)
    corner = first[:, :size]
    pairs = [right(jnp.concatenate([get[0], get[1]], axis=1)) for get in gets]
    squares = []
    for d in range(count):
        both = dot(left(sends[d][1]), pairs[d])
        squares.append(first[:, (d + 1) * size : (d + 2) * size] + both[:, :size])
        corner = corner + both[:, size:]
    cubes = dot(left(corner), row)
    cube = cubes[:, :size]
    for d in range(count):
        uses = sum(jnp.where(c == me + steps[d], 1.0, 0.0) for c in named[1:]).astype(jnp.float32)
        both = uses * dot(left(squares[d]), pairs[d])
        cube = cube + both[:, size:]
        far = cubes[:, (d + 1) * size : (d + 2) * size] + both[:, :size]
        results[d + 1] = 3.0 * squares[d] - 2.0 * far
    results[0] = 3.0 * corner - 2.0 * cube
    results[count + 1] = jnp.zeros((size, size), jnp.float32)
    copies = []
    for s in range(kslots):
        source = jnp.int32(count + 1)
        for d, step in enumerate((0,) + steps):
            source = jnp.where((named[s] >= 0) & (named[s] == me + step), d, source)
        copies.append(
            pltpu.make_async_copy(results.at[source], out.at[0, 0, 0, s], out_sems.at[s])
        )
    for copy in copies:
        copy.start()
    for copy in copies:
        copy.wait()


def on_device(blocks, columns):
    kslots, size = blocks.shape[3], blocks.shape[4]
    columns = jnp.swapaxes(columns, 2, 3)
    steps = strides(columns.shape)
    count = len(steps)
    vmem = pl.BlockSpec(memory_space=pltpu.VMEM)
    hbm = pl.BlockSpec(memory_space=pl.ANY)
    pair = jax.ShapeDtypeStruct((2, size, size), jnp.float32)
    rows = pltpu.SMEM(columns.shape[2:], jnp.int32)
    sends = pl.pallas_call(
        functools.partial(outgoing, steps),
        out_shape=(pair,) * count,
        in_specs=[hbm, vmem],
        out_specs=(vmem,) * count,
        scratch_shapes=[rows, pltpu.SemaphoreType.DMA],
        compiler_params=pltpu.CompilerParams(vmem_limit_bytes=VMEM_BYTES),
        name="outgoing",
    )(columns, blocks)
    gets = [None] * count
    for d, (axis, step) in enumerate(SIDES):
        ends = lax.axis_size(axis)
        pairs = [(i, i + step) for i in range(ends) if 0 <= i + step < ends]
        gets[SIDES.index((axis, -step))] = lax.ppermute(sends[d], axis, pairs)
    return pl.pallas_call(
        functools.partial(finish, steps),
        out_shape=jax.ShapeDtypeStruct(blocks.shape, jnp.float32),
        in_specs=[hbm] + [vmem] * (2 * count),
        out_specs=hbm,
        scratch_shapes=[
            pltpu.VMEM((count + 2, size, size), jnp.float32),
            rows,
            pltpu.SemaphoreType.DMA,
            pltpu.SemaphoreType.DMA((kslots,)),
        ],
        compiler_params=pltpu.CompilerParams(vmem_limit_bytes=VMEM_BYTES),
        name="finish",
    )(columns, *sends, *gets)


def solution(mesh):
    return jax.shard_map(
        on_device,
        mesh=mesh,
        in_specs=(P("gx", "gy", "gz", None, None, None), P()),
        out_specs=P("gx", "gy", "gz", None, None, None),
        check_vma=False,
    )
```

time: 319 us -> 36.4 us (0.11)
  the two profiles are of different devices: /device:TPU:432 before, /device:TPU:46 now
where the time goes in v1:
time: 36.4 us; the launch traced here: 36.1 us
  starting transfers between devices  21.8 us (60%)
  waiting for transfers between devices  9.06 us (25%)
  Pallas kernels  3.22 us (9%)
  local copies, waits for them, and re-layouts  1.94 us (5%)
    ppermute x6, starting transfers between devices, on_device(): gets[SIDES.index((axis, -step))] = lax.ppermute(sends[d], axis, pairs)  21.8 us
    ppermute x6, waiting for transfers between devices, on_device(): gets[SIDES.index((axis, -step))] = lax.ppermute(sends[d], axis, pairs)  9.06 us
    pallas_call x1, Pallas kernels, on_device(): pl.pallas_call(functools.partial(finish, steps), out_shape=jax.ShapeDtype...  2.43 us
    unnamed x4, local copies, waits for them, and re-layouts  1.94 us
    pallas_call x1, Pallas kernels, on_device(): pl.pallas_call(functools.partial(outgoing, steps), out_shape=(pair,) * co...  0.79 us
  transfers between devices with their start and end apart: 6, of which 2 were waited for; matrix products, arithmetic and copies ran while one was open for 0% of the time, Pallas kernels for 0%

profile of v1, /device:TPU:46, one launch (start us, length us, event | category | flops | bytes accessed | tf_op | source)
XLA Modules:
  0.0 36.1 jit_solution(10267785453161122631)
XLA Ops:
  0.0 0.0 copy-start
  0.0 0.9 %copy-done = s32[8,4,16,8]{2,3,1,0:T(8,128)S(1)} copy-done((s32[8,4,16,8]{2,3,1,0:T(8,128)S(1)}, s32[8,4,16,8]{2,3,1,0:T(8,128)}, u32[]{:S(2)}) %copy-start) | copy-done | bytes 16408
  0.9 0.0 copy-start.1
  0.9 1.0 %copy-done.1 = f32[1,1,1,8,128,128]{5,4,3,2,1,0:T(8,128)S(1)} copy-done((f32[1,1,1,8,128,128]{5,4,3,2,1,0:T(8,128)S(1)}, f32[1,1,1,8,128,128]{5,4,3,2,1,0:T(8,128)}, u32[]{:S(2)}) %copy-start.1) | copy-done | bytes 524312
  1.9 0.8 %outgoing.1 = (f32[2,128,128]{2,1,0:T(8,128)S(1)}, f32[2,128,128]{2,1,0:T(8,128)S(1)}, f32[2,128,128]{2,1,0:T(8,128)S(1)}, f32[2,128,128]{2,1,0:T(8,128)S(1)}, f...) custom-call(s32[8,4,8,16]{3,2,1,0:T(8,128)S(1)} %bitcast.1, f32[1,1,1,8,128,128]{5,4,3,2,1,0:T(8,128)S(1)} %copy-done.1), custom_call_target="tpu_custom_call" | custom-call | tf_op jit(solution)/shard_map/outgoing/pallas_call | solution.py:123
  2.7 9.1 %collective-permute-start.1 = (f32[2,128,128]{2,1,0:T(8,128)S(1)}, f32[2,128,128]{2,1,0:T(8,128)S(1)}, u32[]{:S(2)}, u32[]{:S(2)}) collective-permute-start(f32[2,128,128]{2,1,0:T(8,128)S(1)} %get-tuple-element.11.rest_0_), channel_id=1, source_target_pairs={{0,16},{16,32},{32,48},{1,17},{17,33},{33,49},{2,18},{18,34},{34,5... | collective-permute-start | bytes 393224 | tf_op jit(solution)/shard_map/ppermute | solution.py:136
  11.9 1.3 %collective-permute-start = (f32[2,128,128]{2,1,0:T(8,128)S(1)}, f32[2,128,128]{2,1,0:T(8,128)S(1)}, u32[]{:S(2)}, u32[]{:S(2)}) collective-permute-start(f32[2,128,128]{2,1,0:T(8,128)S(1)} %get-tuple-element.12.rest_1_), channel_id=1, source_target_pairs={{16,0},{32,16},{48,32},{17,1},{33,17},{49,33},{18,2},{34,18},{50,3... | collective-permute-start | bytes 393224 | tf_op jit(solution)/shard_map/ppermute | solution.py:136
  13.2 1.9 %collective-permute-start.3 = (f32[2,128,128]{2,1,0:T(8,128)S(1)}, f32[2,128,128]{2,1,0:T(8,128)S(1)}, u32[]{:S(2)}, u32[]{:S(2)}) collective-permute-start(f32[2,128,128]{2,1,0:T(8,128)S(1)} %get-tuple-element.13.rest_2_), channel_id=1, source_target_pairs={{0,64},{64,128},{128,192},{192,256},{256,320},{320,384},{384,448},... | collective-permute-start | bytes 393224 | tf_op jit(solution)/shard_map/ppermute | solution.py:136
  15.1 3.6 %collective-permute-start.2 = (f32[2,128,128]{2,1,0:T(8,128)S(1)}, f32[2,128,128]{2,1,0:T(8,128)S(1)}, u32[]{:S(2)}, u32[]{:S(2)}) collective-permute-start(f32[2,128,128]{2,1,0:T(8,128)S(1)} %get-tuple-element.14.rest_3_), channel_id=1, source_target_pairs={{64,0},{128,64},{192,128},{256,192},{320,256},{384,320},{448,384},... | collective-permute-start | bytes 393224 | tf_op jit(solution)/shard_map/ppermute | solution.py:136
  18.7 3.7 %collective-permute-start.5 = (f32[2,128,128]{2,1,0:T(8,128)S(1)}, f32[2,128,128]{2,1,0:T(8,128)S(1)}, u32[]{:S(2)}, u32[]{:S(2)}) collective-permute-start(f32[2,128,128]{2,1,0:T(8,128)S(1)} %get-tuple-element.15.rest_4_), channel_id=1, source_target_pairs={{0,1},{1,2},{2,3},{3,4},{4,5},{5,6},{6,7},{7,8},{8,9},{9,10},{10,1... | collective-permute-start | bytes 393224 | tf_op jit(solution)/shard_map/ppermute | solution.py:136
  22.5 0.0 collective-permute-done.1.rest_7_
  22.5 2.1 %collective-permute-start.4 = (f32[2,128,128]{2,1,0:T(8,128)S(1)}, f32[2,128,128]{2,1,0:T(8,128)S(1)}, u32[]{:S(2)}, u32[]{:S(2)}) collective-permute-start(f32[2,128,128]{2,1,0:T(8,128)S(1)} %get-tuple-element.16.rest_5_), channel_id=1, source_target_pairs={{1,0},{2,1},{3,2},{4,3},{5,4},{6,5},{7,6},{8,7},{9,8},{10,9},{11,1... | collective-permute-start | bytes 393224 | tf_op jit(solution)/shard_map/ppermute | solution.py:136
  24.6 5.3 %collective-permute-done.rest_6_ = f32[2,128,128]{2,1,0:T(8,128)S(1)} collective-permute-done((f32[2,128,128]{2,1,0:T(8,128)S(1)}, f32[2,128,128]{2,1,0:T(8,128)S(1)}, u32[]{:S(2)}, u32[]{:S(2)}) %collective-permute-start) | collective-permute-done | bytes 131104 | tf_op jit(solution)/shard_map/ppermute | solution.py:136
  29.9 0.0 collective-permute-done.3.rest_9_
  29.9 0.0 collective-permute-done.2.rest_8_
  29.9 0.0 collective-permute-done.5.rest_11_
  29.9 3.7 %collective-permute-done.4.rest_10_ = f32[2,128,128]{2,1,0:T(8,128)S(1)} collective-permute-done((f32[2,128,128]{2,1,0:T(8,128)S(1)}, f32[2,128,128]{2,1,0:T(8,128)S(1)}, u32[]{:S(2)}, u32[]{:S(2)}) %collective-permute-start.4) | collective-permute-done | bytes 131104 | tf_op jit(solution)/shard_map/ppermute | solution.py:136
  33.7 2.4 %finish.1 = f32[1,1,1,8,128,128]{5,4,3,2,1,0:T(8,128)} custom-call(s32[8,4,8,16]{3,2,1,0:T(8,128)S(1)} %bitcast.2, f32[2,128,128]{2,1,0:T(8,128)S(1)} %get-tuple-element.11.rest_0_, f32[2,128,128]{2,1,0:T(8,128)S(1)} %get-tuple-element.12.rest_1_, f32[2,128,128]{2,1,0:T(8,128)S(1)} %get-tuple-element.13.rest_2_, ...), custom_call_target="tpu_custom_call" | custom-call | tf_op jit(solution)/shard_map/finish/pallas_call | solution.py:137
Async XLA Ops:
  0.0 0.9 %copy-start = (s32[8,4,16,8]{2,3,1,0:T(8,128)S(1)}, s32[8,4,16,8]{2,3,1,0:T(8,128)}, u32[]{:S(2)}) copy-start(s32[8,4,16,8]{2,3,1,0:T(8,128)} %param.3) | copy-start | bytes 49156
  0.9 1.0 %copy-start.1 = (f32[1,1,1,8,128,128]{5,4,3,2,1,0:T(8,128)S(1)}, f32[1,1,1,8,128,128]{5,4,3,2,1,0:T(8,128)}, u32[]{:S(2)}) copy-start(f32[1,1,1,8,128,128]{5,4,3,2,1,0:T(8,128)} %blocks.1) | copy-start | bytes 1572868
  2.7 19.7 %collective-permute-start.1 = (f32[2,128,128]{2,1,0:T(8,128)S(1)}, f32[2,128,128]{2,1,0:T(8,128)S(1)}, u32[]{:S(2)}, u32[]{:S(2)}) collective-permute-start(f32[2,128,128]{2,1,0:T(8,128)S(1)} %get-tuple-element.11.rest_0_), channel_id=1, source_target_pairs={{0,16},{16,32},{32,48},{1,17},{17,33},{33,49},{2,18},{18,34},{34,5... | collective-permute-start | bytes 393224 | tf_op jit(solution)/shard_map/ppermute | solution.py:136
  11.9 18.1 %collective-permute-start = (f32[2,128,128]{2,1,0:T(8,128)S(1)}, f32[2,128,128]{2,1,0:T(8,128)S(1)}, u32[]{:S(2)}, u32[]{:S(2)}) collective-permute-start(f32[2,128,128]{2,1,0:T(8,128)S(1)} %get-tuple-element.12.rest_1_), channel_id=1, source_target_pairs={{16,0},{32,16},{48,32},{17,1},{33,17},{49,33},{18,2},{34,18},{50,3... | collective-permute-start | bytes 393224 | tf_op jit(solution)/shard_map/ppermute | solution.py:136
  13.2 16.8 %collective-permute-start.3 = (f32[2,128,128]{2,1,0:T(8,128)S(1)}, f32[2,128,128]{2,1,0:T(8,128)S(1)}, u32[]{:S(2)}, u32[]{:S(2)}) collective-permute-start(f32[2,128,128]{2,1,0:T(8,128)S(1)} %get-tuple-element.13.rest_2_), channel_id=1, source_target_pairs={{0,64},{64,128},{128,192},{192,256},{256,320},{320,384},{384,448},... | collective-permute-start | bytes 393224 | tf_op jit(solution)/shard_map/ppermute | solution.py:136
  15.1 14.9 %collective-permute-start.2 = (f32[2,128,128]{2,1,0:T(8,128)S(1)}, f32[2,128,128]{2,1,0:T(8,128)S(1)}, u32[]{:S(2)}, u32[]{:S(2)}) collective-permute-start(f32[2,128,128]{2,1,0:T(8,128)S(1)} %get-tuple-element.14.rest_3_), channel_id=1, source_target_pairs={{64,0},{128,64},{192,128},{256,192},{320,256},{384,320},{448,384},... | collective-permute-start | bytes 393224 | tf_op jit(solution)/shard_map/ppermute | solution.py:136
  18.7 11.2 %collective-permute-start.5 = (f32[2,128,128]{2,1,0:T(8,128)S(1)}, f32[2,128,128]{2,1,0:T(8,128)S(1)}, u32[]{:S(2)}, u32[]{:S(2)}) collective-permute-start(f32[2,128,128]{2,1,0:T(8,128)S(1)} %get-tuple-element.15.rest_4_), channel_id=1, source_target_pairs={{0,1},{1,2},{2,3},{3,4},{4,5},{5,6},{6,7},{7,8},{8,9},{9,10},{10,1... | collective-permute-start | bytes 393224 | tf_op jit(solution)/shard_map/ppermute | solution.py:136
  22.5 11.2 %collective-permute-start.4 = (f32[2,128,128]{2,1,0:T(8,128)S(1)}, f32[2,128,128]{2,1,0:T(8,128)S(1)}, u32[]{:S(2)}, u32[]{:S(2)}) collective-permute-start(f32[2,128,128]{2,1,0:T(8,128)S(1)} %get-tuple-element.16.rest_5_), channel_id=1, source_target_pairs={{1,0},{2,1},{3,2},{4,3},{5,4},{6,5},{7,6},{8,7},{9,8},{10,9},{11,1... | collective-permute-start | bytes 393224 | tf_op jit(solution)/shard_map/ppermute | solution.py:136

commit v2 on v1

v2 whole, which is shorter than its diff:
```python
import functools

import jax
import jax.numpy as jnp
from jax import lax
from jax.experimental import pallas as pl
from jax.experimental.pallas import tpu as pltpu
from jax.sharding import PartitionSpec as P

SHIFT, SWAP = "shift", "swap"
ROUNDS = (
    ("gz", SWAP, 1),
    ("gy", SHIFT, -1),
    ("gy", SHIFT, 1),
    ("gz", SWAP, 0),
    ("gx", SWAP, 1),
    ("gx", SWAP, 0),
)
VMEM_BYTES = 8 * 1024 * 1024


def moves(round_, count):
    _, kind, which = round_
    if kind == SHIFT:
        return [(i, i + which) for i in range(count) if 0 <= i + which < count]
    firsts = range(which, count - 1, 2)
    return [(i, i + 1) for i in firsts] + [(i + 1, i) for i in firsts]


def place(columns_shape):
    total_x, total_y, _, total_z = columns_shape
    sizes = {"gx": total_x, "gy": total_y, "gz": total_z}
    at = {axis: lax.axis_index(axis) for axis in sizes}
    stride = {"gx": total_y * total_z, "gy": total_z, "gz": 1}
    me = (at["gx"] * total_y + at["gy"]) * total_z + at["gz"]
    partners = []
    for axis, kind, which in ROUNDS:
        step = which
        if kind != SHIFT:
            step = jnp.where(at[axis] % 2 == which, 1, -1)
        there = at[axis] + step
        inside = (there >= 0) & (there < sizes[axis])
        partners.append(jnp.where(inside, me + step * stride[axis], -2))
    return at, me, partners


def bringer(d):
    axis, kind, which = ROUNDS[d]
    return ROUNDS.index((axis, SHIFT, -which)) if kind == SHIFT else d


def fetch_row(columns, rows, sem, at):
    return pltpu.make_async_copy(columns.at[at["gx"], at["gy"]], rows, sem)


def outgoing(parts, columns, blocks, *rest):
    count = len(ROUNDS)
    sends, (uses, held, rows, sem, sems) = rest[:count], rest[count:]
    at, me, partners = place(columns.shape)
    kslots, size = blocks.shape[3], blocks.shape[4]
    height = size // parts
    row = fetch_row(columns, rows, sem, at)
    row.start()
    copies = []
    for n in range(parts):
        part = pl.ds(n * height, height)
        copies.append(
            pltpu.make_async_copy(blocks.at[0, 0, 0, :, part, :], held.at[:, part, :], sems.at[n])
        )
        copies[-1].start()
    row.wait()
    weights = [
        [jnp.where(rows[s, at["gz"]] == partner, 1.0, 0.0).astype(jnp.float32) for s in range(1, kslots)]
        for partner in partners
    ]
    for d, weight in enumerate(weights):
        uses[d] = jnp.full(uses.shape[1:], sum(weight), jnp.float32)
    for n in range(parts):
        copies[n].wait()
        for start in range(n * height, (n + 1) * height, 8):
            part = pl.ds(start, 8)
            own = held[0, part, :]
            others = [held[s, part, :] for s in range(1, kslots)]
            for send, weight in zip(sends, weights):
                send[0, part, :] = own
                send[1, part, :] = sum(w * v for w, v in zip(weight, others))


def halves(value):
    high = value.astype(jnp.bfloat16)
    return high, (value - high.astype(jnp.float32)).astype(jnp.bfloat16)


def left(value):
    high, low = halves(value)
    return jnp.concatenate([high, low, high], axis=1)


def right(value):
    high, low = halves(value)
    return jnp.concatenate([high, high, low], axis=0)


def dot(a, b):
    return jnp.dot(a, b, preferred_element_type=jnp.float32)


def contribute(there, get, straight, uses):
    size = straight.shape[0]
    pair = right(jnp.concatenate([get[0], get[1]], axis=1))
    both = dot(left(there), pair)
    square = straight + both[:, :size]
    twice = dot(left(square), pair)
    return square, both[:, size:], uses * twice[:, :size], uses * twice[:, size:]


def finish(columns, uses, *rest):
    count = len(ROUNDS)
    sends, brought = rest[:count], rest[count : 2 * count]
    out, results, rows, sem, out_sems = rest[2 * count :]
    at, me, partners = place(columns.shape)
    fetch = fetch_row(columns, rows, sem, at)
    fetch.start()
    kslots, size = out.shape[3], out.shape[4]
    own = sends[0][0]
    row = right(jnp.concatenate([own] + [send[1] for send in sends], axis=1))
    first = dot(left(own), row)
    corner = first[:, :size]
    cube = jnp.zeros((size, size), jnp.float32)
    pieces = []
    for d in range(count):
        straight = first[:, (d + 1) * size : (d + 2) * size]
        square, to_corner, far, to_cube = contribute(
            sends[d][1], brought[bringer(d)], straight, uses[d, 0:1, :]
        )
        corner = corner + to_corner
        cube = cube + to_cube
        pieces.append(3.0 * square - 2.0 * far)
    cubes = dot(left(corner), row)
    for d in range(count):
        results[d + 1] = pieces[d] - 2.0 * cubes[:, (d + 1) * size : (d + 2) * size]
    results[0] = 3.0 * corner - 2.0 * (cubes[:, :size] + cube)
    results[count + 1] = jnp.zeros((size, size), jnp.float32)
    fetch.wait()
    copies = []
    for s in range(kslots):
        column = rows[s, at["gz"]]
        source = jnp.int32(count + 1)
        for d, cluster in enumerate([me] + partners):
            source = jnp.where(column == cluster, d, source)
        copies.append(
            pltpu.make_async_copy(results.at[source], out.at[0, 0, 0, s], out_sems.at[s])
        )
    for copy in copies:
        copy.start()
    for copy in copies:
        copy.wait()


def on_device(blocks, columns):
    kslots, size = blocks.shape[3], blocks.shape[4]
    columns = jnp.swapaxes(columns, 2, 3)
    columns = pltpu.with_memory_space_constraint(columns, pltpu.HBM)
    blocks = pltpu.with_memory_space_constraint(blocks, pltpu.HBM)
    count = len(ROUNDS)
    parts = 4
    vmem = pl.BlockSpec(memory_space=pltpu.VMEM)
    hbm = pl.BlockSpec(memory_space=pltpu.HBM)
    params = pltpu.CompilerParams(vmem_limit_bytes=VMEM_BYTES)
    pair = jax.ShapeDtypeStruct((2, size, size), jnp.float32)
    rows = pltpu.SMEM(columns.shape[2:], jnp.int32)
    *sends, uses = pl.pallas_call(
        functools.partial(outgoing, parts),
        out_shape=(pair,) * count + (jax.ShapeDtypeStruct((count, 8, size), jnp.float32),),
        in_specs=[hbm, hbm],
        out_specs=(vmem,) * (count + 1),
        scratch_shapes=[
            pltpu.VMEM((kslots, size, size), jnp.float32),
            rows,
            pltpu.SemaphoreType.DMA,
            pltpu.SemaphoreType.DMA((parts,)),
        ],
        compiler_params=params,
        name="outgoing",
    )(columns, blocks)
    brought = [
        lax.ppermute(send, round_[0], moves(round_, lax.axis_size(round_[0])))
        for round_, send in zip(ROUNDS, sends)
    ]
    return pl.pallas_call(
        finish,
        out_shape=jax.ShapeDtypeStruct(blocks.shape, jnp.float32),
        in_specs=[hbm] + [vmem] * (1 + 2 * count),
        out_specs=hbm,
        scratch_shapes=[
            pltpu.VMEM((count + 2, size, size), jnp.float32),
            rows,
            pltpu.SemaphoreType.DMA,
            pltpu.SemaphoreType.DMA((kslots,)),
        ],
        compiler_params=params,
        name="finish",
    )(columns, uses, *sends, *brought)


def solution(mesh):
    return jax.shard_map(
        on_device,
        mesh=mesh,
        in_specs=(P("gx", "gy", "gz", None, None, None), P()),
        out_specs=P("gx", "gy", "gz", None, None, None),
        check_vma=False,
    )
```

time: 36.4 us -> 31.1 us (0.85)
  the two profiles are of different devices: /device:TPU:46 before, /device:TPU:386 now
where the time goes in v2:
time: 31.1 us; the launch traced here: 30.7 us
  starting transfers between devices  17.6 us (57%)
  waiting for transfers between devices  9.45 us (30%)
  Pallas kernels  3.64 us (12%)
    ppermute x6, starting transfers between devices, on_device(): lax.ppermute(send, round_[0], moves(round_, lax.axis_size(round_[0])))  17.6 us
    ppermute x6, waiting for transfers between devices, on_device(): lax.ppermute(send, round_[0], moves(round_, lax.axis_size(round_[0])))  9.45 us
    pallas_call x1, Pallas kernels, on_device(): pl.pallas_call(finish, out_shape=jax.ShapeDtypeStruct(blocks.shape, jnp.f...  2.46 us
    pallas_call x1, Pallas kernels, on_device(): pl.pallas_call(functools.partial(outgoing, parts), out_shape=(pair,) * co...  1.18 us
  transfers between devices with their start and end apart: 6, of which 2 were waited for; matrix products, arithmetic and copies ran while one was open for 0% of the time, Pallas kernels for 0%

profile of v2, /device:TPU:386, one launch (start us, length us, event | category | flops | bytes accessed | tf_op | source)
XLA Modules:
  0.0 30.7 jit_solution(16115422369785342132)
XLA Ops:
  0.0 1.2 %outgoing.1 = (f32[2,128,128]{2,1,0:T(8,128)S(1)}, f32[2,128,128]{2,1,0:T(8,128)S(1)}, f32[2,128,128]{2,1,0:T(8,128)S(1)}, f32[2,128,128]{2,1,0:T(8,128)S(1)}, f...) custom-call(s32[8,4,8,16]{3,2,1,0:T(8,128)} %bitcast.1, ...), custom_call_target="tpu_custom_call" | custom-call | tf_op jit(solution)/shard_map/outgoing/pallas_call | solution.py:172
  1.2 3.4 %collective-permute-start = (f32[2,128,128]{2,1,0:T(8,128)S(1)}, f32[2,128,128]{2,1,0:T(8,128)S(1)}, u32[]{:S(2)}, u32[]{:S(2)}) collective-permute-start(f32[2,128,128]{2,1,0:T(8,128)S(1)} %get-tuple-element.13.rest_0_), channel_id=1, source_target_pairs={{1,2},{3,4},{5,6},{7,8},{9,10},{11,12},{13,14},{2,1},{4,3},{6,5},{... | collective-permute-start | bytes 393224 | tf_op jit(solution)/shard_map/ppermute | solution.py:187
  4.6 5.5 %collective-permute-start.1 = (f32[2,128,128]{2,1,0:T(8,128)S(1)}, f32[2,128,128]{2,1,0:T(8,128)S(1)}, u32[]{:S(2)}, u32[]{:S(2)}) collective-permute-start(f32[2,128,128]{2,1,0:T(8,128)S(1)} %get-tuple-element.14.rest_1_), channel_id=1, source_target_pairs={{16,0},{32,16},{48,32},{17,1},{33,17},{49,33},{18,2},{34,18},{50,3... | collective-permute-start | bytes 393224 | tf_op jit(solution)/shard_map/ppermute | solution.py:187
  10.1 1.3 %collective-permute-start.2 = (f32[2,128,128]{2,1,0:T(8,128)S(1)}, f32[2,128,128]{2,1,0:T(8,128)S(1)}, u32[]{:S(2)}, u32[]{:S(2)}) collective-permute-start(f32[2,128,128]{2,1,0:T(8,128)S(1)} %get-tuple-element.15.rest_2_), channel_id=1, source_target_pairs={{0,16},{16,32},{32,48},{1,17},{17,33},{33,49},{2,18},{18,34},{34,5... | collective-permute-start | bytes 393224 | tf_op jit(solution)/shard_map/ppermute | solution.py:187
  11.4 1.9 %collective-permute-start.3 = (f32[2,128,128]{2,1,0:T(8,128)S(1)}, f32[2,128,128]{2,1,0:T(8,128)S(1)}, u32[]{:S(2)}, u32[]{:S(2)}) collective-permute-start(f32[2,128,128]{2,1,0:T(8,128)S(1)} %get-tuple-element.16.rest_3_), channel_id=1, source_target_pairs={{0,1},{2,3},{4,5},{6,7},{8,9},{10,11},{12,13},{14,15},{1,0},{3,2},... | collective-permute-start | bytes 393224 | tf_op jit(solution)/shard_map/ppermute | solution.py:187
  13.3 0.7 %collective-permute-start.4 = (f32[2,128,128]{2,1,0:T(8,128)S(1)}, f32[2,128,128]{2,1,0:T(8,128)S(1)}, u32[]{:S(2)}, u32[]{:S(2)}) collective-permute-start(f32[2,128,128]{2,1,0:T(8,128)S(1)} %get-tuple-element.17.rest_4_), channel_id=1, source_target_pairs={{64,128},{192,256},{320,384},{128,64},{256,192},{384,320},{65,129}... | collective-permute-start | bytes 393224 | tf_op jit(solution)/shard_map/ppermute | solution.py:187
  14.0 0.0 collective-permute-done.rest_6_
  14.0 4.8 %collective-permute-start.5 = (f32[2,128,128]{2,1,0:T(8,128)S(1)}, f32[2,128,128]{2,1,0:T(8,128)S(1)}, u32[]{:S(2)}, u32[]{:S(2)}) collective-permute-start(f32[2,128,128]{2,1,0:T(8,128)S(1)} %get-tuple-element.18.rest_5_), channel_id=1, source_target_pairs={{0,64},{128,192},{256,320},{384,448},{64,0},{192,128},{320,256},{4... | collective-permute-start | bytes 393224 | tf_op jit(solution)/shard_map/ppermute | solution.py:187
  18.8 2.1 %collective-permute-done.1.rest_7_ = f32[2,128,128]{2,1,0:T(8,128)S(1)} collective-permute-done((f32[2,128,128]{2,1,0:T(8,128)S(1)}, f32[2,128,128]{2,1,0:T(8,128)S(1)}, u32[]{:S(2)}, u32[]{:S(2)}) %collective-permute-start.1) | collective-permute-done | bytes 131104 | tf_op jit(solution)/shard_map/ppermute | solution.py:187
  20.9 7.3 %collective-permute-done.2.rest_8_ = f32[2,128,128]{2,1,0:T(8,128)S(1)} collective-permute-done((f32[2,128,128]{2,1,0:T(8,128)S(1)}, f32[2,128,128]{2,1,0:T(8,128)S(1)}, u32[]{:S(2)}, u32[]{:S(2)}) %collective-permute-start.2) | collective-permute-done | bytes 131104 | tf_op jit(solution)/shard_map/ppermute | solution.py:187
  28.3 0.0 collective-permute-done.3.rest_9_
  28.3 0.0 collective-permute-done.4.rest_10_
  28.3 0.0 collective-permute-done.5.rest_11_
  28.3 2.5 %finish.1 = f32[1,1,1,8,128,128]{5,4,3,2,1,0:T(8,128)} custom-call(s32[8,4,8,16]{3,2,1,0:T(8,128)} %bitcast.2, f32[6,8,128]{2,1,0:T(8,128)S(1)} %get-tuple-element.12.uses, f32[2,128,128]{2,1,0:T(8,128)S(1)} %get-tuple-element.13.rest_0_, f32[2,128,128]{2,1,0:T(8,128)S(1)} %get-tuple-element.14.rest_1_, f32[2,128,128]{2,1,0:T(8,128)S(1)} %get-tuple-element.15.rest_2_, ...), custom_call_target="tpu_custom_call" | custom-call | tf_op jit(solution)/shard_map/finish/pallas_call | solution.py:190
Async XLA Ops:
  1.2 12.8 %collective-permute-start = (f32[2,128,128]{2,1,0:T(8,128)S(1)}, f32[2,128,128]{2,1,0:T(8,128)S(1)}, u32[]{:S(2)}, u32[]{:S(2)}) collective-permute-start(f32[2,128,128]{2,1,0:T(8,128)S(1)} %get-tuple-element.13.rest_0_), channel_id=1, source_target_pairs={{1,2},{3,4},{5,6},{7,8},{9,10},{11,12},{13,14},{2,1},{4,3},{6,5},{... | collective-permute-start | bytes 393224 | tf_op jit(solution)/shard_map/ppermute | solution.py:187
  4.6 16.3 %collective-permute-start.1 = (f32[2,128,128]{2,1,0:T(8,128)S(1)}, f32[2,128,128]{2,1,0:T(8,128)S(1)}, u32[]{:S(2)}, u32[]{:S(2)}) collective-permute-start(f32[2,128,128]{2,1,0:T(8,128)S(1)} %get-tuple-element.14.rest_1_), channel_id=1, source_target_pairs={{16,0},{32,16},{48,32},{17,1},{33,17},{49,33},{18,2},{34,18},{50,3... | collective-permute-start | bytes 393224 | tf_op jit(solution)/shard_map/ppermute | solution.py:187
  10.1 18.2 %collective-permute-start.2 = (f32[2,128,128]{2,1,0:T(8,128)S(1)}, f32[2,128,128]{2,1,0:T(8,128)S(1)}, u32[]{:S(2)}, u32[]{:S(2)}) collective-permute-start(f32[2,128,128]{2,1,0:T(8,128)S(1)} %get-tuple-element.15.rest_2_), channel_id=1, source_target_pairs={{0,16},{16,32},{32,48},{1,17},{17,33},{33,49},{2,18},{18,34},{34,5... | collective-permute-start | bytes 393224 | tf_op jit(solution)/shard_map/ppermute | solution.py:187
  11.4 16.9 %collective-permute-start.3 = (f32[2,128,128]{2,1,0:T(8,128)S(1)}, f32[2,128,128]{2,1,0:T(8,128)S(1)}, u32[]{:S(2)}, u32[]{:S(2)}) collective-permute-start(f32[2,128,128]{2,1,0:T(8,128)S(1)} %get-tuple-element.16.rest_3_), channel_id=1, source_target_pairs={{0,1},{2,3},{4,5},{6,7},{8,9},{10,11},{12,13},{14,15},{1,0},{3,2},... | collective-permute-start | bytes 393224 | tf_op jit(solution)/shard_map/ppermute | solution.py:187
  13.3 15.0 %collective-permute-start.4 = (f32[2,128,128]{2,1,0:T(8,128)S(1)}, f32[2,128,128]{2,1,0:T(8,128)S(1)}, u32[]{:S(2)}, u32[]{:S(2)}) collective-permute-start(f32[2,128,128]{2,1,0:T(8,128)S(1)} %get-tuple-element.17.rest_4_), channel_id=1, source_target_pairs={{64,128},{192,256},{320,384},{128,64},{256,192},{384,320},{65,129}... | collective-permute-start | bytes 393224 | tf_op jit(solution)/shard_map/ppermute | solution.py:187
  14.0 14.3 %collective-permute-start.5 = (f32[2,128,128]{2,1,0:T(8,128)S(1)}, f32[2,128,128]{2,1,0:T(8,128)S(1)}, u32[]{:S(2)}, u32[]{:S(2)}) collective-permute-start(f32[2,128,128]{2,1,0:T(8,128)S(1)} %get-tuple-element.18.rest_5_), channel_id=1, source_target_pairs={{0,64},{128,192},{256,320},{384,448},{64,0},{192,128},{320,256},{4... | collective-permute-start | bytes 393224 | tf_op jit(solution)/shard_map/ppermute | solution.py:187

commit v3 on v2

--- a/solution.py
+++ b/solution.py
@@ -7,46 +7,69 @@
 from jax.experimental.pallas import tpu as pltpu
 from jax.sharding import PartitionSpec as P
 
-SHIFT, SWAP = "shift", "swap"
+X_EVEN, X_ODD, Y_EVEN, Y_ODD, Z_EVEN, Z_ODD = SWAPS = (
+    ("gx", 0),
+    ("gx", 1),
+    ("gy", 0),
+    ("gy", 1),
+    ("gz", 0),
+    ("gz", 1),
+)
+AXES = ("gx", "gy", "gz")
 ROUNDS = (
-    ("gz", SWAP, 1),
-    ("gy", SHIFT, -1),
-    ("gy", SHIFT, 1),
-    ("gz", SWAP, 0),
-    ("gx", SWAP, 1),
-    ("gx", SWAP, 0),
+    (Y_EVEN, Y_EVEN, None, X_ODD),
+    (Z_EVEN, Y_ODD, Y_ODD, None),
+    (Z_ODD, Z_ODD, Y_EVEN, Y_EVEN),
+    (X_EVEN, Z_EVEN, Z_ODD, Z_ODD),
+    (X_ODD, X_ODD, X_ODD, Z_EVEN),
+    (None, X_EVEN, Z_EVEN, None),
+    (None, None, X_EVEN, X_EVEN),
 )
 VMEM_BYTES = 8 * 1024 * 1024
 
 
-def moves(round_, count):
-    _, kind, which = round_
-    if kind == SHIFT:
-        return [(i, i + which) for i in range(count) if 0 <= i + which < count]
-    firsts = range(which, count - 1, 2)
-    return [(i, i + 1) for i in firsts] + [(i + 1, i) for i in firsts]
+def partner_of(at, sizes, swap):
+    axis, which = swap
+    there = dict(at)
+    there[axis] += 1 if at[axis] % 2 == which else -1
+    return there if 0 <= there[axis] < sizes[axis] else None
+
+
+def moves(round_, sizes):
+    def index(at):
+        return (at["gx"] * sizes["gy"] + at["gy"]) * sizes["gz"] + at["gz"]
+
+    pairs = []
+    for x in range(sizes["gx"]):
+        for y in range(sizes["gy"]):
+            for z in range(sizes["gz"]):
+                at = {"gx": x, "gy": y, "gz": z}
+                there = round_[y] and partner_of(at, sizes, round_[y])
+                if there:
+                    pairs.append((index(at), index(there)))
+    return pairs
 
 
 def place(columns_shape):
     total_x, total_y, _, total_z = columns_shape
     sizes = {"gx": total_x, "gy": total_y, "gz": total_z}
-    at = {axis: lax.axis_index(axis) for axis in sizes}
+    at = {axis: lax.axis_index(axis) for axis in AXES}
     stride = {"gx": total_y * total_z, "gy": total_z, "gz": 1}
     me = (at["gx"] * total_y + at["gy"]) * total_z + at["gz"]
-    partners = []
-    for axis, kind, which in ROUNDS:
-        step = which
-        if kind != SHIFT:
-            step = jnp.where(at[axis] % 2 == which, 1, -1)
+    by_swap = {None: jnp.int32(-2)}
+    for axis, which in SWAPS:
+        step = jnp.where(at[axis] % 2 == which, 1, -1)
         there = at[axis] + step
         inside = (there >= 0) & (there < sizes[axis])
-        partners.append(jnp.where(inside, me + step * stride[axis], -2))
+        by_swap[axis, which] = jnp.where(inside, me + step * stride[axis], -2)
+    partners = []
+    for round_ in ROUNDS:
+        partner = by_swap[round_[0]]
+        for y in range(1, total_y):
+            if any(round_[y] != round_[0] for y in range(1, total_y)):
+                partner = jnp.where(at["gy"] == y, by_swap[round_[y]], partner)
+        partners.append(partner)
     return at, me, partners
-
-
-def bringer(d):
-    axis, kind, which = ROUNDS[d]
-    return ROUNDS.index((axis, SHIFT, -which)) if kind == SHIFT else d
 
 
 def fetch_row(columns, rows, sem, at):
@@ -73,8 +96,10 @@
         [jnp.where(rows[s, at["gz"]] == partner, 1.0, 0.0).astype(jnp.float32) for s in range(1, kslots)]
         for partner in partners
     ]
+    lanes = uses.shape[2]
     for d, weight in enumerate(weights):
-        uses[d] = jnp.full(uses.shape[1:], sum(weight), jnp.float32)
+        for s, value in enumerate([sum(weight)] + weight):
+            uses[d, s : s + 1, :] = jnp.full((1, lanes), value, jnp.float32)
     for n in range(parts):
         copies[n].wait()
         for start in range(n * height, (n + 1) * height, 8):
@@ -114,13 +139,10 @@
     return square, both[:, size:], uses * twice[:, :size], uses * twice[:, size:]
 
 
-def finish(columns, uses, *rest):
+def finish(uses, *rest):
     count = len(ROUNDS)
     sends, brought = rest[:count], rest[count : 2 * count]
-    out, results, rows, sem, out_sems = rest[2 * count :]
-    at, me, partners = place(columns.shape)
-    fetch = fetch_row(columns, rows, sem, at)
-    fetch.start()
+    out, results, slots, out_sems = rest[2 * count :]
     kslots, size = out.shape[3], out.shape[4]
     own = sends[0][0]
     row = right(jnp.concatenate([own] + [send[1] for send in sends], axis=1))
@@ -131,28 +153,27 @@
     for d in range(count):
         straight = first[:, (d + 1) * size : (d + 2) * size]
         square, to_corner, far, to_cube = contribute(
-            sends[d][1], brought[bringer(d)], straight, uses[d, 0:1, :]
+            sends[d][1], brought[d], straight, uses[d, 0:1, :]
         )
         corner = corner + to_corner
         cube = cube + to_cube
         pieces.append(3.0 * square - 2.0 * far)
     cubes = dot(left(corner), row)
+    copies = [
+        pltpu.make_async_copy(slots.at[s], out.at[0, 0, 0, s], out_sems.at[s]) for s in range(kslots)
+    ]
+    slots[0] = 3.0 * corner - 2.0 * (cubes[:, :size] + cube)
+    copies[0].start()
     for d in range(count):
-        results[d + 1] = pieces[d] - 2.0 * cubes[:, (d + 1) * size : (d + 2) * size]
-    results[0] = 3.0 * corner - 2.0 * (cubes[:, :size] + cube)
-    results[count + 1] = jnp.zeros((size, size), jnp.float32)
-    fetch.wait()
-    copies = []
-    for s in range(kslots):
-        column = rows[s, at["gz"]]
-        source = jnp.int32(count + 1)
-        for d, cluster in enumerate([me] + partners):
-            source = jnp.where(column == cluster, d, source)
-        copies.append(
-            pltpu.make_async_copy(results.at[source], out.at[0, 0, 0, s], out_sems.at[s])
-        )
-    for copy in copies:
-        copy.start()
+        results[d] = pieces[d] - 2.0 * cubes[:, (d + 1) * size : (d + 2) * size]
+    for s in range(1, kslots):
+        for start in range(0, size, 8):
+            part = pl.ds(start, 8)
+            value = jnp.zeros((8, size), jnp.float32)
+            for d in range(count):
+                value = jnp.where(uses[d, s : s + 1, :] > 0.0, results[d, part, :], value)
+            slots[s, part, :] = value
+        copies[s].start()
     for copy in copies:
         copy.wait()
 
@@ -183,24 +204,21 @@
         compiler_params=params,
         name="outgoing",
     )(columns, blocks)
-    brought = [
-        lax.ppermute(send, round_[0], moves(round_, lax.axis_size(round_[0])))
-        for round_, send in zip(ROUNDS, sends)
-    ]
+    sizes = {axis: lax.axis_size(axis) for axis in AXES}
+    brought = [lax.ppermute(send, AXES, moves(round_, sizes)) for round_, send in zip(ROUNDS, sends)]
     return pl.pallas_call(
         finish,
         out_shape=jax.ShapeDtypeStruct(blocks.shape, jnp.float32),
-        in_specs=[hbm] + [vmem] * (1 + 2 * count),
+        in_specs=[vmem] * (1 + 2 * count),
         out_specs=hbm,
         scratch_shapes=[
-            pltpu.VMEM((count + 2, size, size), jnp.float32),
-            rows,
-            pltpu.SemaphoreType.DMA,
+            pltpu.VMEM((count, size, size), jnp.float32),
+            pltpu.VMEM((kslots, size, size), jnp.float32),
             pltpu.SemaphoreType.DMA((kslots,)),
         ],
         compiler_params=params,
         name="finish",
-    )(columns, uses, *sends, *brought)
+    )(uses, *sends, *brought)
 
 
 def solution(mesh):

time: 31.1 us -> 29.9 us (0.961)
  the two profiles are of different devices: /device:TPU:386 before, /device:TPU:184 now
where the time goes in v3:
time: 29.9 us; the launch traced here: 29.6 us
  starting transfers between devices  20.4 us (68%)
  waiting for transfers between devices  5.85 us (20%)
  Pallas kernels  3.29 us (11%)
    ppermute x7, starting transfers between devices, on_device(): lax.ppermute(send, AXES, moves(round_, sizes))  20.4 us
    ppermute x7, waiting for transfers between devices, on_device(): lax.ppermute(send, AXES, moves(round_, sizes))  5.85 us
    pallas_call x1, Pallas kernels, on_device(): pl.pallas_call(finish, out_shape=jax.ShapeDtypeStruct(blocks.shape, jnp.f...  2.09 us
    pallas_call x1, Pallas kernels, on_device(): pl.pallas_call(functools.partial(outgoing, parts), out_shape=(pair,) * co...  1.19 us
  transfers between devices with their start and end apart: 7, of which 2 were waited for; matrix products, arithmetic and copies ran while one was open for 0% of the time, Pallas kernels for 0%

profile of v3, /device:TPU:184, one launch (start us, length us, event | category | flops | bytes accessed | tf_op | source)
XLA Modules:
  0.0 29.6 jit_solution(16883896609902507040)
XLA Ops:
  0.0 1.2 %outgoing.1 = (f32[2,128,128]{2,1,0:T(8,128)S(1)}, f32[2,128,128]{2,1,0:T(8,128)S(1)}, f32[2,128,128]{2,1,0:T(8,128)S(1)}, f32[2,128,128]{2,1,0:T(8,128)S(1)}, f...) custom-call(s32[8,4,8,16]{3,2,1,0:T(8,128)} %bitcast.1, ...), custom_call_target="tpu_custom_call" | custom-call | tf_op jit(solution)/shard_map/outgoing/pallas_call | solution.py:193
  1.2 1.9 %collective-permute-start = (f32[2,128,128]{2,1,0:T(8,128)S(1)}, f32[2,128,128]{2,1,0:T(8,128)S(1)}, u32[]{:S(2)}, u32[]{:S(2)}) collective-permute-start(f32[2,128,128]{2,1,0:T(8,128)S(1)} %get-tuple-element.14.rest_0_), channel_id=1, source_target_pairs={{0,16},{1,17},{2,18},{3,19},{4,20},{5,21},{6,22},{7,23},{8,24},{9,... | collective-permute-start | bytes 393224 | tf_op jit(solution)/shard_map/ppermute | solution.py:208
  3.1 6.9 %collective-permute-start.1 = (f32[2,128,128]{2,1,0:T(8,128)S(1)}, f32[2,128,128]{2,1,0:T(8,128)S(1)}, u32[]{:S(2)}, u32[]{:S(2)}) collective-permute-start(f32[2,128,128]{2,1,0:T(8,128)S(1)} %get-tuple-element.15.rest_1_), channel_id=1, source_target_pairs={{0,1},{1,0},{2,3},{3,2},{4,5},{5,4},{6,7},{7,6},{8,9},{9,8},{10,11... | collective-permute-start | bytes 393224 | tf_op jit(solution)/shard_map/ppermute | solution.py:208
  10.1 5.1 %collective-permute-start.2 = (f32[2,128,128]{2,1,0:T(8,128)S(1)}, f32[2,128,128]{2,1,0:T(8,128)S(1)}, u32[]{:S(2)}, u32[]{:S(2)}) collective-permute-start(f32[2,128,128]{2,1,0:T(8,128)S(1)} %get-tuple-element.16.rest_2_), channel_id=1, source_target_pairs={{1,2},{2,1},{3,4},{4,3},{5,6},{6,5},{7,8},{8,7},{9,10},{10,9},{11,... | collective-permute-start | bytes 393224 | tf_op jit(solution)/shard_map/ppermute | solution.py:208
  15.2 1.9 %collective-permute-start.3 = (f32[2,128,128]{2,1,0:T(8,128)S(1)}, f32[2,128,128]{2,1,0:T(8,128)S(1)}, u32[]{:S(2)}, u32[]{:S(2)}) collective-permute-start(f32[2,128,128]{2,1,0:T(8,128)S(1)} %get-tuple-element.17.rest_3_), channel_id=1, source_target_pairs={{0,64},{1,65},{2,66},{3,67},{4,68},{5,69},{6,70},{7,71},{8,72},{9,... | collective-permute-start | bytes 393224 | tf_op jit(solution)/shard_map/ppermute | solution.py:208
  17.1 1.9 %collective-permute-start.4 = (f32[2,128,128]{2,1,0:T(8,128)S(1)}, f32[2,128,128]{2,1,0:T(8,128)S(1)}, u32[]{:S(2)}, u32[]{:S(2)}) collective-permute-start(f32[2,128,128]{2,1,0:T(8,128)S(1)} %get-tuple-element.18.rest_4_), channel_id=1, source_target_pairs={{48,49},{49,48},{50,51},{51,50},{52,53},{53,52},{54,55},{55,54},{5... | collective-permute-start | bytes 393224 | tf_op jit(solution)/shard_map/ppermute | solution.py:208
  19.1 0.0 collective-permute-done.rest_7_
  19.1 1.9 %collective-permute-start.5 = (f32[2,128,128]{2,1,0:T(8,128)S(1)}, f32[2,128,128]{2,1,0:T(8,128)S(1)}, u32[]{:S(2)}, u32[]{:S(2)}) collective-permute-start(f32[2,128,128]{2,1,0:T(8,128)S(1)} %get-tuple-element.19.rest_5_), channel_id=1, source_target_pairs={{16,80},{17,81},{18,82},{19,83},{20,84},{21,85},{22,86},{23,87},{2... | collective-permute-start | bytes 393224 | tf_op jit(solution)/shard_map/ppermute | solution.py:208
  21.0 1.1 %collective-permute-done.1.rest_8_ = f32[2,128,128]{2,1,0:T(8,128)S(1)} collective-permute-done((f32[2,128,128]{2,1,0:T(8,128)S(1)}, f32[2,128,128]{2,1,0:T(8,128)S(1)}, u32[]{:S(2)}, u32[]{:S(2)}) %collective-permute-start.1) | collective-permute-done | bytes 131104 | tf_op jit(solution)/shard_map/ppermute | solution.py:208
  22.1 0.7 %collective-permute-start.6 = (f32[2,128,128]{2,1,0:T(8,128)S(1)}, f32[2,128,128]{2,1,0:T(8,128)S(1)}, u32[]{:S(2)}, u32[]{:S(2)}) collective-permute-start(f32[2,128,128]{2,1,0:T(8,128)S(1)} %get-tuple-element.20.rest_6_), channel_id=1, source_target_pairs={{32,96},{33,97},{34,98},{35,99},{36,100},{37,101},{38,102},{39,103... | collective-permute-start | bytes 393224 | tf_op jit(solution)/shard_map/ppermute | solution.py:208
  22.8 4.7 %collective-permute-done.2.rest_9_ = f32[2,128,128]{2,1,0:T(8,128)S(1)} collective-permute-done((f32[2,128,128]{2,1,0:T(8,128)S(1)}, f32[2,128,128]{2,1,0:T(8,128)S(1)}, u32[]{:S(2)}, u32[]{:S(2)}) %collective-permute-start.2) | collective-permute-done | bytes 131104 | tf_op jit(solution)/shard_map/ppermute | solution.py:208
  27.5 0.0 collective-permute-done.3.rest_10_
  27.5 0.0 collective-permute-done.4.rest_11_
  27.5 0.0 collective-permute-done.5.rest_12_
  27.5 0.0 collective-permute-done.6.rest_13_
  27.5 2.1 %finish.1 = f32[1,1,1,8,128,128]{5,4,3,2,1,0:T(8,128)} custom-call(f32[7,8,128]{2,1,0:T(8,128)S(1)} %get-tuple-element.13.uses, f32[2,128,128]{2,1,0:T(8,128)S(1)} %get-tuple-element.14.rest_0_, f32[2,128,128]{2,1,0:T(8,128)S(1)} %get-tuple-element.15.rest_1_, f32[2,128,128]{2,1,0:T(8,128)S(1)} %get-tuple-element.16.rest_2_, ...), custom_call_target="tpu_custom_call" | custom-call | tf_op jit(solution)/shard_map/finish/pallas_call | solution.py:209
Async XLA Ops:
  1.2 17.9 %collective-permute-start = (f32[2,128,128]{2,1,0:T(8,128)S(1)}, f32[2,128,128]{2,1,0:T(8,128)S(1)}, u32[]{:S(2)}, u32[]{:S(2)}) collective-permute-start(f32[2,128,128]{2,1,0:T(8,128)S(1)} %get-tuple-element.14.rest_0_), channel_id=1, source_target_pairs={{0,16},{1,17},{2,18},{3,19},{4,20},{5,21},{6,22},{7,23},{8,24},{9,... | collective-permute-start | bytes 393224 | tf_op jit(solution)/shard_map/ppermute | solution.py:208
  3.1 19.0 %collective-permute-start.1 = (f32[2,128,128]{2,1,0:T(8,128)S(1)}, f32[2,128,128]{2,1,0:T(8,128)S(1)}, u32[]{:S(2)}, u32[]{:S(2)}) collective-permute-start(f32[2,128,128]{2,1,0:T(8,128)S(1)} %get-tuple-element.15.rest_1_), channel_id=1, source_target_pairs={{0,1},{1,0},{2,3},{3,2},{4,5},{5,4},{6,7},{7,6},{8,9},{9,8},{10,11... | collective-permute-start | bytes 393224 | tf_op jit(solution)/shard_map/ppermute | solution.py:208
  10.1 17.4 %collective-permute-start.2 = (f32[2,128,128]{2,1,0:T(8,128)S(1)}, f32[2,128,128]{2,1,0:T(8,128)S(1)}, u32[]{:S(2)}, u32[]{:S(2)}) collective-permute-start(f32[2,128,128]{2,1,0:T(8,128)S(1)} %get-tuple-element.16.rest_2_), channel_id=1, source_target_pairs={{1,2},{2,1},{3,4},{4,3},{5,6},{6,5},{7,8},{8,7},{9,10},{10,9},{11,... | collective-permute-start | bytes 393224 | tf_op jit(solution)/shard_map/ppermute | solution.py:208
  15.2 12.3 %collective-permute-start.3 = (f32[2,128,128]{2,1,0:T(8,128)S(1)}, f32[2,128,128]{2,1,0:T(8,128)S(1)}, u32[]{:S(2)}, u32[]{:S(2)}) collective-permute-start(f32[2,128,128]{2,1,0:T(8,128)S(1)} %get-tuple-element.17.rest_3_), channel_id=1, source_target_pairs={{0,64},{1,65},{2,66},{3,67},{4,68},{5,69},{6,70},{7,71},{8,72},{9,... | collective-permute-start | bytes 393224 | tf_op jit(solution)/shard_map/ppermute | solution.py:208
  17.1 10.4 %collective-permute-start.4 = (f32[2,128,128]{2,1,0:T(8,128)S(1)}, f32[2,128,128]{2,1,0:T(8,128)S(1)}, u32[]{:S(2)}, u32[]{:S(2)}) collective-permute-start(f32[2,128,128]{2,1,0:T(8,128)S(1)} %get-tuple-element.18.rest_4_), channel_id=1, source_target_pairs={{48,49},{49,48},{50,51},{51,50},{52,53},{53,52},{54,55},{55,54},{5... | collective-permute-start | bytes 393224 | tf_op jit(solution)/shard_map/ppermute | solution.py:208
  19.1 8.4 %collective-permute-start.5 = (f32[2,128,128]{2,1,0:T(8,128)S(1)}, f32[2,128,128]{2,1,0:T(8,128)S(1)}, u32[]{:S(2)}, u32[]{:S(2)}) collective-permute-start(f32[2,128,128]{2,1,0:T(8,128)S(1)} %get-tuple-element.19.rest_5_), channel_id=1, source_target_pairs={{16,80},{17,81},{18,82},{19,83},{20,84},{21,85},{22,86},{23,87},{2... | collective-permute-start | bytes 393224 | tf_op jit(solution)/shard_map/ppermute | solution.py:208
  22.1 5.4 %collective-permute-start.6 = (f32[2,128,128]{2,1,0:T(8,128)S(1)}, f32[2,128,128]{2,1,0:T(8,128)S(1)}, u32[]{:S(2)}, u32[]{:S(2)}) collective-permute-start(f32[2,128,128]{2,1,0:T(8,128)S(1)} %get-tuple-element.20.rest_6_), channel_id=1, source_target_pairs={{32,96},{33,97},{34,98},{35,99},{36,100},{37,101},{38,102},{39,103... | collective-permute-start | bytes 393224 | tf_op jit(solution)/shard_map/ppermute | solution.py:208

commit v4 on v3

v4 whole, which is shorter than its diff:
```python
import functools

import jax
import jax.numpy as jnp
import numpy as np
from jax import lax
from jax.experimental import pallas as pl
from jax.experimental.pallas import tpu as pltpu
from jax.sharding import PartitionSpec as P

SCHEDULE = (
    (
        "yXzZx..", "yXzZx..", "yXzZx..", "yZzXx..", "yZzXx..", "yXzZx..", "yXzZx..", "yZzXx..",
        "yZzXx..", "yXzZx..", "yXzZx..", "yZzXx..", "yZzXx..", "yXzZx..", "yXzZx..", "yXzZx..",
    ),
    (
        "yYXzZx.", "yYXzZx.", "yYXzZx.", "yZYzXx.", "yZYzXx.", "yYXzZx.", "yYXzZx.", "yZYzXx.",
        "yZYzXx.", "yYXzZx.", "yYXzZx.", "yZYzXx.", "yZYzXx.", "yYXzZx.", "yYXzZx.", "yYXzZx.",
    ),
    (
        ".YyXZzx", ".YyXZzx", ".YyXZzx", "Z.YyXzx", "Z.YyXzx", ".YyXZzx", ".YyXZzx", "Z.YyXzx",
        "Z.YyXzx", ".YyXZzx", ".YyXZzx", "Z.YyXzx", "Z.YyXzx", ".YyXZzx", ".YyXZzx", ".YyXZzx",
    ),
    (
        "X.yxZz.", "X.yxZz.", "X.yxZz.", "Z..yXzx", "Z..yXzx", "X.yxZz.", "X.yxZz.", "Z..yXzx",
        "Z..yXzx", "X.yxZz.", "X.yxZz.", "Z..yXzx", "Z..yXzx", "X.yxZz.", "X.yxZz.", "X.yxZz.",
    ),
)
ROUNDS = range(len(SCHEDULE[0][0]))
AXES = ("gx", "gy", "gz")
LETTERS = {"x": 0, "y": 1, "z": 2}
EARLY = 2
VMEM_BYTES = 8 * 1024 * 1024


def partners_of(sizes):
    table = np.full((len(ROUNDS),) + sizes, -2, np.int32)
    for at in np.ndindex(sizes):
        for n, letter in enumerate(SCHEDULE[at[1]][at[2]]):
            if letter == ".":
                continue
            axis = LETTERS[letter.lower()]
            there = list(at)
            there[axis] += 1 if at[axis] % 2 == letter.isupper() else -1
            if 0 <= there[axis] < sizes[axis]:
                table[(n,) + at] = np.ravel_multi_index(there, sizes)
    return table


def fetch_row(table, rows, sem):
    place = table.at[lax.axis_index("gx"), lax.axis_index("gy")]
    return pltpu.make_async_copy(place, rows, sem)


def outgoing(parts, columns, partners, blocks, *rest):
    count = len(ROUNDS)
    sends, (uses, held, rows, near, row_sems, sems) = rest[:count], rest[count:]
    kslots, size = blocks.shape[3], blocks.shape[4]
    height = size // parts
    fetches = [
        fetch_row(columns, rows, row_sems.at[0]),
        fetch_row(partners, near, row_sems.at[1]),
    ]
    for fetch in fetches:
        fetch.start()
    copies = []
    for n in range(parts):
        part = pl.ds(n * height, height)
        copies.append(
            pltpu.make_async_copy(blocks.at[0, 0, 0, :, part, :], held.at[:, part, :], sems.at[n])
        )
        copies[-1].start()
    for fetch in fetches:
        fetch.wait()
    z = lax.axis_index("gz")
    named = [rows[s, z] for s in range(1, kslots)]
    weights = [
        [jnp.where(column == near[n, z], 1.0, 0.0).astype(jnp.float32) for column in named]
        for n in ROUNDS
    ]
    lanes = uses.shape[2]
    for d, weight in enumerate(weights):
        for s, value in enumerate([sum(weight)] + weight):
            uses[d, s : s + 1, :] = jnp.full((1, lanes), value, jnp.float32)
    for n in range(parts):
        copies[n].wait()
        for start in range(n * height, (n + 1) * height, 8):
            part = pl.ds(start, 8)
            own = held[0, part, :]
            others = [held[s, part, :] for s in range(1, kslots)]
            for send, weight in zip(sends, weights):
                send[0, part, :] = own
                send[1, part, :] = sum(w * v for w, v in zip(weight, others))


def halves(value):
    high = value.astype(jnp.bfloat16)
    return high, (value - high.astype(jnp.float32)).astype(jnp.bfloat16)


def left(value):
    high, low = halves(value)
    return jnp.concatenate([high, low, high], axis=1)


def right(value):
    high, low = halves(value)
    return jnp.concatenate([high, high, low], axis=0)


def dot(a, b):
    return jnp.dot(a, b, preferred_element_type=jnp.float32)


def contribute(there, get, straight, uses):
    size = straight.shape[0]
    pair = right(jnp.concatenate([get[0], get[1]], axis=1))
    both = dot(left(there), pair)
    square = straight + both[:, :size]
    twice = dot(left(square), pair)
    return square, both[:, size:], uses * twice[:, :size], uses * twice[:, size:]


def early(uses, *rest):
    count = len(ROUNDS)
    sends, brought = rest[:count], rest[count : count + EARLY]
    partial, row_out = rest[count + EARLY :]
    size = partial.shape[1]
    own = sends[0][0]
    row = right(jnp.concatenate([own] + [send[1] for send in sends], axis=1))
    row_out[...] = row
    first = dot(left(own), row)
    corner = first[:, :size]
    cube = jnp.zeros((size, size), jnp.float32)
    for d in range(count):
        straight = first[:, (d + 1) * size : (d + 2) * size]
        if d < EARLY:
            square, to_corner, far, to_cube = contribute(
                sends[d][1], brought[d], straight, uses[d, 0:1, :]
            )
            corner = corner + to_corner
            cube = cube + to_cube
            straight = 3.0 * square - 2.0 * far
        partial[d] = straight
    partial[count] = corner
    partial[count + 1] = cube


def finish(uses, partial, row_in, *rest):
    count = len(ROUNDS)
    late = count - EARLY
    sends, brought = rest[:late], rest[late : 2 * late]
    out, results, slots, out_sems = rest[2 * late :]
    kslots, size = out.shape[3], out.shape[4]
    corner = partial[count]
    cube = partial[count + 1]
    pieces = [partial[d] for d in range(count)]
    for d in range(EARLY, count):
        square, to_corner, far, to_cube = contribute(
            sends[d - EARLY][1], brought[d - EARLY], pieces[d], uses[d, 0:1, :]
        )
        corner = corner + to_corner
        cube = cube + to_cube
        pieces[d] = 3.0 * square - 2.0 * far
    cubes = dot(left(corner), row_in[...])
    copies = [
        pltpu.make_async_copy(slots.at[s], out.at[0, 0, 0, s], out_sems.at[s]) for s in range(kslots)
    ]
    slots[0] = 3.0 * corner - 2.0 * (cubes[:, :size] + cube)
    copies[0].start()
    for d in range(count):
        results[d] = pieces[d] - 2.0 * cubes[:, (d + 1) * size : (d + 2) * size]
    for s in range(1, kslots):
        for start in range(0, size, 8):
            part = pl.ds(start, 8)
            value = jnp.zeros((8, size), jnp.float32)
            for d in range(count):
                value = jnp.where(uses[d, s : s + 1, :] > 0.0, results[d, part, :], value)
            slots[s, part, :] = value
        copies[s].start()
    for copy in copies:
        copy.wait()


def on_device(blocks, columns):
    kslots, size = blocks.shape[3], blocks.shape[4]
    columns = jnp.swapaxes(columns, 2, 3)
    sizes = tuple(lax.axis_size(axis) for axis in AXES)
    table = partners_of(sizes)
    partners = jnp.asarray(table.transpose(1, 2, 0, 3))
    columns = pltpu.with_memory_space_constraint(columns, pltpu.HBM)
    partners = pltpu.with_memory_space_constraint(partners, pltpu.HBM)
    blocks = pltpu.with_memory_space_constraint(blocks, pltpu.HBM)
    count = len(ROUNDS)
    parts = 4
    vmem = pl.BlockSpec(memory_space=pltpu.VMEM)
    hbm = pl.BlockSpec(memory_space=pltpu.HBM)
    params = pltpu.CompilerParams(vmem_limit_bytes=VMEM_BYTES)
    pair = jax.ShapeDtypeStruct((2, size, size), jnp.float32)
    *sends, uses = pl.pallas_call(
        functools.partial(outgoing, parts),
        out_shape=(pair,) * count + (jax.ShapeDtypeStruct((count, 8, size), jnp.float32),),
        in_specs=[hbm, hbm, hbm],
        out_specs=(vmem,) * (count + 1),
        scratch_shapes=[
            pltpu.VMEM((kslots, size, size), jnp.float32),
            pltpu.SMEM(columns.shape[2:], jnp.int32),
            pltpu.SMEM(partners.shape[2:], jnp.int32),
            pltpu.SemaphoreType.DMA((2,)),
            pltpu.SemaphoreType.DMA((parts,)),
        ],
        compiler_params=params,
        name="outgoing",
    )(columns, partners, blocks)
    brought = [
        lax.ppermute(send, AXES, [(i, int(j)) for i, j in enumerate(row.ravel()) if j >= 0])
        for row, send in zip(table, sends)
    ]
    partial, row = pl.pallas_call(
        early,
        out_shape=(
            jax.ShapeDtypeStruct((count + 2, size, size), jnp.float32),
            jax.ShapeDtypeStruct((3 * size, (count + 1) * size), jnp.bfloat16),
        ),
        in_specs=[vmem] * (1 + count + EARLY),
        out_specs=(vmem, vmem),
        compiler_params=params,
        name="early",
    )(uses, *sends, *brought[:EARLY])
    return pl.pallas_call(
        finish,
        out_shape=jax.ShapeDtypeStruct(blocks.shape, jnp.float32),
        in_specs=[vmem] * (3 + 2 * (count - EARLY)),
        out_specs=hbm,
        scratch_shapes=[
            pltpu.VMEM((count, size, size), jnp.float32),
            pltpu.VMEM((kslots, size, size), jnp.float32),
            pltpu.SemaphoreType.DMA((kslots,)),
        ],
        compiler_params=params,
        name="finish",
    )(uses, partial, row, *sends[EARLY:], *brought[EARLY:])


def solution(mesh):
    return jax.shard_map(
        on_device,
        mesh=mesh,
        in_specs=(P("gx", "gy", "gz", None, None, None), P()),
        out_specs=P("gx", "gy", "gz", None, None, None),
        check_vma=False,
    )
```

time: 29.9 us -> 29.3 us (0.980)
  the two profiles are of different devices: /device:TPU:184 before, /device:TPU:256 now
where the time goes in v4:
time: 29.3 us; the launch traced here: 29 us
  starting transfers between devices  15 us (51%)
  waiting for transfers between devices  10.2 us (35%)
  Pallas kernels  3.69 us (13%)
    ppermute x7, starting transfers between devices, on_device(): lax.ppermute(send, AXES, [(i, int(j)) for i, j in enumerate(row.ravel())...  15 us
    ppermute x7, waiting for transfers between devices, on_device(): lax.ppermute(send, AXES, [(i, int(j)) for i, j in enumerate(row.ravel())...  10.2 us
    pallas_call x1, Pallas kernels, on_device(): pl.pallas_call(finish, out_shape=jax.ShapeDtypeStruct(blocks.shape, jnp.f...  1.82 us
    pallas_call x1, Pallas kernels, on_device(): pl.pallas_call(functools.partial(outgoing, parts), out_shape=(pair,) * co...  1.26 us
    pallas_call x1, Pallas kernels, on_device(): pl.pallas_call(early, out_shape=(jax.ShapeDtypeStruct((count + 2, size, s...  0.62 us
  transfers between devices with their start and end apart: 7, of which 2 were waited for; matrix products, arithmetic and copies ran while one was open for 0% of the time, Pallas kernels for 2%

profile of v4, /device:TPU:256, one launch (start us, length us, event | category | flops | bytes accessed | tf_op | source)
XLA Modules:
  0.0 29.0 jit_solution(5441179814093101218)
XLA Ops:
  0.0 1.3 %outgoing.1 = (f32[2,128,128]{2,1,0:T(8,128)S(1)}, f32[2,128,128]{2,1,0:T(8,128)S(1)}, f32[2,128,128]{2,1,0:T(8,128)S(1)}, f32[2,128,128]{2,1,0:T(8,128)S(1)}, f...) custom-call(s32[8,4,8,16]{3,2,1,0:T(8,128)} %bitcast.1, ...), custom_call_target="tpu_custom_call" | custom-call | tf_op jit(solution)/shard_map/outgoing/pallas_call | solution.py:200
  1.3 0.7 %collective-permute-start = (f32[2,128,128]{2,1,0:T(8,128)S(1)}, f32[2,128,128]{2,1,0:T(8,128)S(1)}, u32[]{:S(2)}, u32[]{:S(2)}) collective-permute-start(f32[2,128,128]{2,1,0:T(8,128)S(1)} %get-tuple-element.16.rest_0_), channel_id=1, source_target_pairs={{0,16},{1,17},{2,18},{3,19},{4,20},{5,21},{6,22},{7,23},{8,24},{9,... | collective-permute-start | bytes 393224 | tf_op jit(solution)/shard_map/ppermute | solution.py:216
  1.9 6.0 %collective-permute-start.1 = (f32[2,128,128]{2,1,0:T(8,128)S(1)}, f32[2,128,128]{2,1,0:T(8,128)S(1)}, u32[]{:S(2)}, u32[]{:S(2)}) collective-permute-start(f32[2,128,128]{2,1,0:T(8,128)S(1)} %get-tuple-element.17.rest_1_), channel_id=1, source_target_pairs={{3,4},{4,3},{7,8},{8,7},{11,12},{12,11},{16,32},{17,33},{18,34},{1... | collective-permute-start | bytes 393224 | tf_op jit(solution)/shard_map/ppermute | solution.py:216
  8.0 1.9 %collective-permute-start.2 = (f32[2,128,128]{2,1,0:T(8,128)S(1)}, f32[2,128,128]{2,1,0:T(8,128)S(1)}, u32[]{:S(2)}, u32[]{:S(2)}) collective-permute-start(f32[2,128,128]{2,1,0:T(8,128)S(1)} %get-tuple-element.18.rest_2_.rest_0_), channel_id=1, source_target_pairs={{0,1},{1,0},{2,3},{3,2},{4,5},{5,4},{6,7},{7,6},{8,9},{9,8},{10,11... | collective-permute-start | bytes 393224 | tf_op jit(solution)/shard_map/ppermute | solution.py:216
  9.9 0.7 %collective-permute-start.3 = (f32[2,128,128]{2,1,0:T(8,128)S(1)}, f32[2,128,128]{2,1,0:T(8,128)S(1)}, u32[]{:S(2)}, u32[]{:S(2)}) collective-permute-start(f32[2,128,128]{2,1,0:T(8,128)S(1)} %get-tuple-element.19.rest_3_.rest_1_), channel_id=1, source_target_pairs={{1,2},{2,1},{5,6},{6,5},{9,10},{10,9},{13,14},{14,13},{16,17},{17,... | collective-permute-start | bytes 393224 | tf_op jit(solution)/shard_map/ppermute | solution.py:216
  10.6 0.7 %collective-permute-start.4 = (f32[2,128,128]{2,1,0:T(8,128)S(1)}, f32[2,128,128]{2,1,0:T(8,128)S(1)}, u32[]{:S(2)}, u32[]{:S(2)}) collective-permute-start(f32[2,128,128]{2,1,0:T(8,128)S(1)} %get-tuple-element.20.rest_4_.rest_2_), channel_id=1, source_target_pairs={{0,64},{1,65},{2,66},{3,67},{4,68},{5,69},{6,70},{7,71},{8,72},{9,... | collective-permute-start | bytes 393224 | tf_op jit(solution)/shard_map/ppermute | solution.py:216
  11.2 0.0 collective-permute-done.rest_7_
  11.3 3.2 %collective-permute-start.5 = (f32[2,128,128]{2,1,0:T(8,128)S(1)}, f32[2,128,128]{2,1,0:T(8,128)S(1)}, u32[]{:S(2)}, u32[]{:S(2)}) collective-permute-start(f32[2,128,128]{2,1,0:T(8,128)S(1)} %get-tuple-element.21.rest_5_.rest_3_), channel_id=1, source_target_pairs={{16,80},{17,81},{18,82},{19,83},{20,84},{21,85},{22,86},{23,87},{2... | collective-permute-start | bytes 393224 | tf_op jit(solution)/shard_map/ppermute | solution.py:216
  14.4 6.9 %collective-permute-done.1.rest_8_ = f32[2,128,128]{2,1,0:T(8,128)S(1)} collective-permute-done((f32[2,128,128]{2,1,0:T(8,128)S(1)}, f32[2,128,128]{2,1,0:T(8,128)S(1)}, u32[]{:S(2)}, u32[]{:S(2)}) %collective-permute-start.1) | collective-permute-done | bytes 131104 | tf_op jit(solution)/shard_map/ppermute | solution.py:216
  21.3 1.9 %collective-permute-start.6 = (f32[2,128,128]{2,1,0:T(8,128)S(1)}, f32[2,128,128]{2,1,0:T(8,128)S(1)}, u32[]{:S(2)}, u32[]{:S(2)}) collective-permute-start(f32[2,128,128]{2,1,0:T(8,128)S(1)} %get-tuple-element.22.rest_6_.rest_4_), channel_id=1, source_target_pairs={{32,96},{33,97},{34,98},{35,99},{36,100},{37,101},{38,102},{39,103... | collective-permute-start | bytes 393224 | tf_op jit(solution)/shard_map/ppermute | solution.py:216
  23.2 0.6 %early.1 = (f32[9,128,128]{2,1,0:T(8,128)S(1)}, bf16[384,1024]{1,0:T(8,128)(2,1)S(1)}) custom-call(f32[7,8,128]{2,1,0:T(8,128)S(1)} %get-tuple-element.15.uses, f32[2,128,128]{2,1,0:T(8,128)S(1)} %get-tuple-element.16.rest_0_, f32[2,128,128]{2,1,0:T(8,128)S(1)} %get-tuple-element.17.rest_1_, f32[2,128,128]{2,1,0:T(8,128)S(1)} %get-tuple-element.18.rest_2_.rest_0_, ...), custom_call_target="tpu_custom_call" | custom-call | tf_op jit(solution)/shard_map/early/pallas_call | solution.py:219
  23.9 3.3 %collective-permute-done.2.rest_5_ = f32[2,128,128]{2,1,0:T(8,128)S(1)} collective-permute-done((f32[2,128,128]{2,1,0:T(8,128)S(1)}, f32[2,128,128]{2,1,0:T(8,128)S(1)}, u32[]{:S(2)}, u32[]{:S(2)}) %collective-permute-start.2) | collective-permute-done | bytes 131104 | tf_op jit(solution)/shard_map/ppermute | solution.py:216
  27.2 0.0 collective-permute-done.3.rest_6_
  27.2 0.0 collective-permute-done.4.rest_7_
  27.2 0.0 collective-permute-done.5.rest_8_
  27.2 0.0 collective-permute-done.6.rest_9_
  27.2 1.8 %finish.1 = f32[1,1,1,8,128,128]{5,4,3,2,1,0:T(8,128)} custom-call(f32[7,8,128]{2,1,0:T(8,128)S(1)} %get-tuple-element.15.uses, f32[9,128,128]{2,1,0:T(8,128)S(1)} %get-tuple-element.23.partial, bf16[384,1024]{1,0:T(8,128)(2,1)S(1)} %get-tuple-element.24.row_in, f32[2,128,128]{2,1,0:T(8,128)S(1)} %get-tuple-element.18.rest_2_.rest_0_, ...), custom_call_target="tpu_custom_call" | custom-call | tf_op jit(solution)/shard_map/finish/pallas_call | solution.py:230
Async XLA Ops:
  1.3 10.0 %collective-permute-start = (f32[2,128,128]{2,1,0:T(8,128)S(1)}, f32[2,128,128]{2,1,0:T(8,128)S(1)}, u32[]{:S(2)}, u32[]{:S(2)}) collective-permute-start(f32[2,128,128]{2,1,0:T(8,128)S(1)} %get-tuple-element.16.rest_0_), channel_id=1, source_target_pairs={{0,16},{1,17},{2,18},{3,19},{4,20},{5,21},{6,22},{7,23},{8,24},{9,... | collective-permute-start | bytes 393224 | tf_op jit(solution)/shard_map/ppermute | solution.py:216
  1.9 19.4 %collective-permute-start.1 = (f32[2,128,128]{2,1,0:T(8,128)S(1)}, f32[2,128,128]{2,1,0:T(8,128)S(1)}, u32[]{:S(2)}, u32[]{:S(2)}) collective-permute-start(f32[2,128,128]{2,1,0:T(8,128)S(1)} %get-tuple-element.17.rest_1_), channel_id=1, source_target_pairs={{3,4},{4,3},{7,8},{8,7},{11,12},{12,11},{16,32},{17,33},{18,34},{1... | collective-permute-start | bytes 393224 | tf_op jit(solution)/shard_map/ppermute | solution.py:216
  8.0 19.2 %collective-permute-start.2 = (f32[2,128,128]{2,1,0:T(8,128)S(1)}, f32[2,128,128]{2,1,0:T(8,128)S(1)}, u32[]{:S(2)}, u32[]{:S(2)}) collective-permute-start(f32[2,128,128]{2,1,0:T(8,128)S(1)} %get-tuple-element.18.rest_2_.rest_0_), channel_id=1, source_target_pairs={{0,1},{1,0},{2,3},{3,2},{4,5},{5,4},{6,7},{7,6},{8,9},{9,8},{10,11... | collective-permute-start | bytes 393224 | tf_op jit(solution)/shard_map/ppermute | solution.py:216
  9.9 17.3 %collective-permute-start.3 = (f32[2,128,128]{2,1,0:T(8,128)S(1)}, f32[2,128,128]{2,1,0:T(8,128)S(1)}, u32[]{:S(2)}, u32[]{:S(2)}) collective-permute-start(f32[2,128,128]{2,1,0:T(8,128)S(1)} %get-tuple-element.19.rest_3_.rest_1_), channel_id=1, source_target_pairs={{1,2},{2,1},{5,6},{6,5},{9,10},{10,9},{13,14},{14,13},{16,17},{17,... | collective-permute-start | bytes 393224 | tf_op jit(solution)/shard_map/ppermute | solution.py:216
  10.6 16.6 %collective-permute-start.4 = (f32[2,128,128]{2,1,0:T(8,128)S(1)}, f32[2,128,128]{2,1,0:T(8,128)S(1)}, u32[]{:S(2)}, u32[]{:S(2)}) collective-permute-start(f32[2,128,128]{2,1,0:T(8,128)S(1)} %get-tuple-element.20.rest_4_.rest_2_), channel_id=1, source_target_pairs={{0,64},{1,65},{2,66},{3,67},{4,68},{5,69},{6,70},{7,71},{8,72},{9,... | collective-permute-start | bytes 393224 | tf_op jit(solution)/shard_map/ppermute | solution.py:216
  11.3 15.9 %collective-permute-start.5 = (f32[2,128,128]{2,1,0:T(8,128)S(1)}, f32[2,128,128]{2,1,0:T(8,128)S(1)}, u32[]{:S(2)}, u32[]{:S(2)}) collective-permute-start(f32[2,128,128]{2,1,0:T(8,128)S(1)} %get-tuple-element.21.rest_5_.rest_3_), channel_id=1, source_target_pairs={{16,80},{17,81},{18,82},{19,83},{20,84},{21,85},{22,86},{23,87},{2... | collective-permute-start | bytes 393224 | tf_op jit(solution)/shard_map/ppermute | solution.py:216
  21.3 5.9 %collective-permute-start.6 = (f32[2,128,128]{2,1,0:T(8,128)S(1)}, f32[2,128,128]{2,1,0:T(8,128)S(1)}, u32[]{:S(2)}, u32[]{:S(2)}) collective-permute-start(f32[2,128,128]{2,1,0:T(8,128)S(1)} %get-tuple-element.22.rest_6_.rest_4_), channel_id=1, source_target_pairs={{32,96},{33,97},{34,98},{35,99},{36,100},{37,101},{38,102},{39,103... | collective-permute-start | bytes 393224 | tf_op jit(solution)/shard_map/ppermute | solution.py:216

commit v5 on v4

--- a/solution.py
+++ b/solution.py
@@ -192,7 +192,7 @@
     partners = pltpu.with_memory_space_constraint(partners, pltpu.HBM)
     blocks = pltpu.with_memory_space_constraint(blocks, pltpu.HBM)
     count = len(ROUNDS)
-    parts = 4
+    parts = 1
     vmem = pl.BlockSpec(memory_space=pltpu.VMEM)
     hbm = pl.BlockSpec(memory_space=pltpu.HBM)
     params = pltpu.CompilerParams(vmem_limit_bytes=VMEM_BYTES)

time: 29.3 us -> 29.3 us (level)
  no operation moved by 1% of the time
where the time goes in v5:
time: 29.3 us; the launch traced here: 29 us
  starting transfers between devices  15 us (51%)
  waiting for transfers between devices  10.2 us (35%)
  Pallas kernels  3.71 us (13%)
    ppermute x7, starting transfers between devices, on_device(): lax.ppermute(send, AXES, [(i, int(j)) for i, j in enumerate(row.ravel())...  15 us
    ppermute x7, waiting for transfers between devices, on_device(): lax.ppermute(send, AXES, [(i, int(j)) for i, j in enumerate(row.ravel())...  10.2 us
    pallas_call x1, Pallas kernels, on_device(): pl.pallas_call(finish, out_shape=jax.ShapeDtypeStruct(blocks.shape, jnp.f...  1.82 us
    pallas_call x1, Pallas kernels, on_device(): pl.pallas_call(functools.partial(outgoing, parts), out_shape=(pair,) * co...  1.27 us
    pallas_call x1, Pallas kernels, on_device(): pl.pallas_call(early, out_shape=(jax.ShapeDtypeStruct((count + 2, size, s...  0.62 us
  transfers between devices with their start and end apart: 7, of which 2 were waited for; matrix products, arithmetic and copies ran while one was open for 0% of the time, Pallas kernels for 2%

profile of v5, /device:TPU:256, one launch (start us, length us, event | category | flops | bytes accessed | tf_op | source)
XLA Modules:
  0.0 29.0 jit_solution(10815747048222988935)
XLA Ops:
  0.0 1.3 %outgoing.1 = (f32[2,128,128]{2,1,0:T(8,128)S(1)}, f32[2,128,128]{2,1,0:T(8,128)S(1)}, f32[2,128,128]{2,1,0:T(8,128)S(1)}, f32[2,128,128]{2,1,0:T(8,128)S(1)}, f...) custom-call(s32[8,4,8,16]{3,2,1,0:T(8,128)} %bitcast.1, ...), custom_call_target="tpu_custom_call" | custom-call | tf_op jit(solution)/shard_map/outgoing/pallas_call | solution.py:200
  1.3 0.7 %collective-permute-start = (f32[2,128,128]{2,1,0:T(8,128)S(1)}, f32[2,128,128]{2,1,0:T(8,128)S(1)}, u32[]{:S(2)}, u32[]{:S(2)}) collective-permute-start(f32[2,128,128]{2,1,0:T(8,128)S(1)} %get-tuple-element.16.rest_0_), channel_id=1, source_target_pairs={{0,16},{1,17},{2,18},{3,19},{4,20},{5,21},{6,22},{7,23},{8,24},{9,... | collective-permute-start | bytes 393224 | tf_op jit(solution)/shard_map/ppermute | solution.py:216
  2.0 6.0 %collective-permute-start.1 = (f32[2,128,128]{2,1,0:T(8,128)S(1)}, f32[2,128,128]{2,1,0:T(8,128)S(1)}, u32[]{:S(2)}, u32[]{:S(2)}) collective-permute-start(f32[2,128,128]{2,1,0:T(8,128)S(1)} %get-tuple-element.17.rest_1_), channel_id=1, source_target_pairs={{3,4},{4,3},{7,8},{8,7},{11,12},{12,11},{16,32},{17,33},{18,34},{1... | collective-permute-start | bytes 393224 | tf_op jit(solution)/shard_map/ppermute | solution.py:216
  8.0 1.9 %collective-permute-start.2 = (f32[2,128,128]{2,1,0:T(8,128)S(1)}, f32[2,128,128]{2,1,0:T(8,128)S(1)}, u32[]{:S(2)}, u32[]{:S(2)}) collective-permute-start(f32[2,128,128]{2,1,0:T(8,128)S(1)} %get-tuple-element.18.rest_2_.rest_0_), channel_id=1, source_target_pairs={{0,1},{1,0},{2,3},{3,2},{4,5},{5,4},{6,7},{7,6},{8,9},{9,8},{10,11... | collective-permute-start | bytes 393224 | tf_op jit(solution)/shard_map/ppermute | solution.py:216
  9.9 0.7 %collective-permute-start.3 = (f32[2,128,128]{2,1,0:T(8,128)S(1)}, f32[2,128,128]{2,1,0:T(8,128)S(1)}, u32[]{:S(2)}, u32[]{:S(2)}) collective-permute-start(f32[2,128,128]{2,1,0:T(8,128)S(1)} %get-tuple-element.19.rest_3_.rest_1_), channel_id=1, source_target_pairs={{1,2},{2,1},{5,6},{6,5},{9,10},{10,9},{13,14},{14,13},{16,17},{17,... | collective-permute-start | bytes 393224 | tf_op jit(solution)/shard_map/ppermute | solution.py:216
  10.6 0.7 %collective-permute-start.4 = (f32[2,128,128]{2,1,0:T(8,128)S(1)}, f32[2,128,128]{2,1,0:T(8,128)S(1)}, u32[]{:S(2)}, u32[]{:S(2)}) collective-permute-start(f32[2,128,128]{2,1,0:T(8,128)S(1)} %get-tuple-element.20.rest_4_.rest_2_), channel_id=1, source_target_pairs={{0,64},{1,65},{2,66},{3,67},{4,68},{5,69},{6,70},{7,71},{8,72},{9,... | collective-permute-start | bytes 393224 | tf_op jit(solution)/shard_map/ppermute | solution.py:216
  11.3 0.0 collective-permute-done.rest_7_
  11.3 3.2 %collective-permute-start.5 = (f32[2,128,128]{2,1,0:T(8,128)S(1)}, f32[2,128,128]{2,1,0:T(8,128)S(1)}, u32[]{:S(2)}, u32[]{:S(2)}) collective-permute-start(f32[2,128,128]{2,1,0:T(8,128)S(1)} %get-tuple-element.21.rest_5_.rest_3_), channel_id=1, source_target_pairs={{16,80},{17,81},{18,82},{19,83},{20,84},{21,85},{22,86},{23,87},{2... | collective-permute-start | bytes 393224 | tf_op jit(solution)/shard_map/ppermute | solution.py:216
  14.4 6.9 %collective-permute-done.1.rest_8_ = f32[2,128,128]{2,1,0:T(8,128)S(1)} collective-permute-done((f32[2,128,128]{2,1,0:T(8,128)S(1)}, f32[2,128,128]{2,1,0:T(8,128)S(1)}, u32[]{:S(2)}, u32[]{:S(2)}) %collective-permute-start.1) | collective-permute-done | bytes 131104 | tf_op jit(solution)/shard_map/ppermute | solution.py:216
  21.3 1.9 %collective-permute-start.6 = (f32[2,128,128]{2,1,0:T(8,128)S(1)}, f32[2,128,128]{2,1,0:T(8,128)S(1)}, u32[]{:S(2)}, u32[]{:S(2)}) collective-permute-start(f32[2,128,128]{2,1,0:T(8,128)S(1)} %get-tuple-element.22.rest_6_.rest_4_), channel_id=1, source_target_pairs={{32,96},{33,97},{34,98},{35,99},{36,100},{37,101},{38,102},{39,103... | collective-permute-start | bytes 393224 | tf_op jit(solution)/shard_map/ppermute | solution.py:216
  23.2 0.6 %early.1 = (f32[9,128,128]{2,1,0:T(8,128)S(1)}, bf16[384,1024]{1,0:T(8,128)(2,1)S(1)}) custom-call(f32[7,8,128]{2,1,0:T(8,128)S(1)} %get-tuple-element.15.uses, f32[2,128,128]{2,1,0:T(8,128)S(1)} %get-tuple-element.16.rest_0_, f32[2,128,128]{2,1,0:T(8,128)S(1)} %get-tuple-element.17.rest_1_, f32[2,128,128]{2,1,0:T(8,128)S(1)} %get-tuple-element.18.rest_2_.rest_0_, ...), custom_call_target="tpu_custom_call" | custom-call | tf_op jit(solution)/shard_map/early/pallas_call | solution.py:219
  23.9 3.3 %collective-permute-done.2.rest_5_ = f32[2,128,128]{2,1,0:T(8,128)S(1)} collective-permute-done((f32[2,128,128]{2,1,0:T(8,128)S(1)}, f32[2,128,128]{2,1,0:T(8,128)S(1)}, u32[]{:S(2)}, u32[]{:S(2)}) %collective-permute-start.2) | collective-permute-done | bytes 131104 | tf_op jit(solution)/shard_map/ppermute | solution.py:216
  27.2 0.0 collective-permute-done.3.rest_6_
  27.2 0.0 collective-permute-done.4.rest_7_
  27.2 0.0 collective-permute-done.5.rest_8_
  27.2 0.0 collective-permute-done.6.rest_9_
  27.2 1.8 %finish.1 = f32[1,1,1,8,128,128]{5,4,3,2,1,0:T(8,128)} custom-call(f32[7,8,128]{2,1,0:T(8,128)S(1)} %get-tuple-element.15.uses, f32[9,128,128]{2,1,0:T(8,128)S(1)} %get-tuple-element.23.partial, bf16[384,1024]{1,0:T(8,128)(2,1)S(1)} %get-tuple-element.24.row_in, f32[2,128,128]{2,1,0:T(8,128)S(1)} %get-tuple-element.18.rest_2_.rest_0_, ...), custom_call_target="tpu_custom_call" | custom-call | tf_op jit(solution)/shard_map/finish/pallas_call | solution.py:230
Async XLA Ops:
  1.3 10.0 %collective-permute-start = (f32[2,128,128]{2,1,0:T(8,128)S(1)}, f32[2,128,128]{2,1,0:T(8,128)S(1)}, u32[]{:S(2)}, u32[]{:S(2)}) collective-permute-start(f32[2,128,128]{2,1,0:T(8,128)S(1)} %get-tuple-element.16.rest_0_), channel_id=1, source_target_pairs={{0,16},{1,17},{2,18},{3,19},{4,20},{5,21},{6,22},{7,23},{8,24},{9,... | collective-permute-start | bytes 393224 | tf_op jit(solution)/shard_map/ppermute | solution.py:216
  2.0 19.4 %collective-permute-start.1 = (f32[2,128,128]{2,1,0:T(8,128)S(1)}, f32[2,128,128]{2,1,0:T(8,128)S(1)}, u32[]{:S(2)}, u32[]{:S(2)}) collective-permute-start(f32[2,128,128]{2,1,0:T(8,128)S(1)} %get-tuple-element.17.rest_1_), channel_id=1, source_target_pairs={{3,4},{4,3},{7,8},{8,7},{11,12},{12,11},{16,32},{17,33},{18,34},{1... | collective-permute-start | bytes 393224 | tf_op jit(solution)/shard_map/ppermute | solution.py:216
  8.0 19.2 %collective-permute-start.2 = (f32[2,128,128]{2,1,0:T(8,128)S(1)}, f32[2,128,128]{2,1,0:T(8,128)S(1)}, u32[]{:S(2)}, u32[]{:S(2)}) collective-permute-start(f32[2,128,128]{2,1,0:T(8,128)S(1)} %get-tuple-element.18.rest_2_.rest_0_), channel_id=1, source_target_pairs={{0,1},{1,0},{2,3},{3,2},{4,5},{5,4},{6,7},{7,6},{8,9},{9,8},{10,11... | collective-permute-start | bytes 393224 | tf_op jit(solution)/shard_map/ppermute | solution.py:216
  9.9 17.3 %collective-permute-start.3 = (f32[2,128,128]{2,1,0:T(8,128)S(1)}, f32[2,128,128]{2,1,0:T(8,128)S(1)}, u32[]{:S(2)}, u32[]{:S(2)}) collective-permute-start(f32[2,128,128]{2,1,0:T(8,128)S(1)} %get-tuple-element.19.rest_3_.rest_1_), channel_id=1, source_target_pairs={{1,2},{2,1},{5,6},{6,5},{9,10},{10,9},{13,14},{14,13},{16,17},{17,... | collective-permute-start | bytes 393224 | tf_op jit(solution)/shard_map/ppermute | solution.py:216
  10.6 16.6 %collective-permute-start.4 = (f32[2,128,128]{2,1,0:T(8,128)S(1)}, f32[2,128,128]{2,1,0:T(8,128)S(1)}, u32[]{:S(2)}, u32[]{:S(2)}) collective-permute-start(f32[2,128,128]{2,1,0:T(8,128)S(1)} %get-tuple-element.20.rest_4_.rest_2_), channel_id=1, source_target_pairs={{0,64},{1,65},{2,66},{3,67},{4,68},{5,69},{6,70},{7,71},{8,72},{9,... | collective-permute-start | bytes 393224 | tf_op jit(solution)/shard_map/ppermute | solution.py:216
  11.3 15.9 %collective-permute-start.5 = (f32[2,128,128]{2,1,0:T(8,128)S(1)}, f32[2,128,128]{2,1,0:T(8,128)S(1)}, u32[]{:S(2)}, u32[]{:S(2)}) collective-permute-start(f32[2,128,128]{2,1,0:T(8,128)S(1)} %get-tuple-element.21.rest_5_.rest_3_), channel_id=1, source_target_pairs={{16,80},{17,81},{18,82},{19,83},{20,84},{21,85},{22,86},{23,87},{2... | collective-permute-start | bytes 393224 | tf_op jit(solution)/shard_map/ppermute | solution.py:216
  21.3 5.9 %collective-permute-start.6 = (f32[2,128,128]{2,1,0:T(8,128)S(1)}, f32[2,128,128]{2,1,0:T(8,128)S(1)}, u32[]{:S(2)}, u32[]{:S(2)}) collective-permute-start(f32[2,128,128]{2,1,0:T(8,128)S(1)} %get-tuple-element.22.rest_6_.rest_4_), channel_id=1, source_target_pairs={{32,96},{33,97},{34,98},{35,99},{36,100},{37,101},{38,102},{39,103... | collective-permute-start | bytes 393224 | tf_op jit(solution)/shard_map/ppermute | solution.py:216

commit v6 on v4

--- a/solution.py
+++ b/solution.py
@@ -171,11 +171,12 @@
     for d in range(count):
         results[d] = pieces[d] - 2.0 * cubes[:, (d + 1) * size : (d + 2) * size]
     for s in range(1, kslots):
+        named = [jnp.broadcast_to(uses[d, s : s + 1, :], (8, size)) > 0.0 for d in range(count)]
         for start in range(0, size, 8):
             part = pl.ds(start, 8)
             value = jnp.zeros((8, size), jnp.float32)
             for d in range(count):
-                value = jnp.where(uses[d, s : s + 1, :] > 0.0, results[d, part, :], value)
+                value = jnp.where(named[d], results[d, part, :], value)
             slots[s, part, :] = value
         copies[s].start()
     for copy in copies:

time: 29.3 us -> 29.2 us (level)
  no operation moved by 1% of the time
where the time goes in v6:
time: 29.2 us; the launch traced here: 28.9 us
  starting transfers between devices  15 us (51%)
  waiting for transfers between devices  10.2 us (35%)
  Pallas kernels  3.58 us (12%)
    ppermute x7, starting transfers between devices, on_device(): lax.ppermute(send, AXES, [(i, int(j)) for i, j in enumerate(row.ravel())...  15 us
    ppermute x7, waiting for transfers between devices, on_device(): lax.ppermute(send, AXES, [(i, int(j)) for i, j in enumerate(row.ravel())...  10.2 us
    pallas_call x1, Pallas kernels, on_device(): pl.pallas_call(finish, out_shape=jax.ShapeDtypeStruct(blocks.shape, jnp.f...  1.71 us
    pallas_call x1, Pallas kernels, on_device(): pl.pallas_call(functools.partial(outgoing, parts), out_shape=(pair,) * co...  1.26 us
    pallas_call x1, Pallas kernels, on_device(): pl.pallas_call(early, out_shape=(jax.ShapeDtypeStruct((count + 2, size, s...  0.62 us
  transfers between devices with their start and end apart: 7, of which 2 were waited for; matrix products, arithmetic and copies ran while one was open for 0% of the time, Pallas kernels for 2%

profile of v6, /device:TPU:256, one launch (start us, length us, event | category | flops | bytes accessed | tf_op | source)
XLA Modules:
  0.0 28.9 jit_solution(2437317819092853822)
XLA Ops:
  0.0 1.3 %outgoing.1 = (f32[2,128,128]{2,1,0:T(8,128)S(1)}, f32[2,128,128]{2,1,0:T(8,128)S(1)}, f32[2,128,128]{2,1,0:T(8,128)S(1)}, f32[2,128,128]{2,1,0:T(8,128)S(1)}, f...) custom-call(s32[8,4,8,16]{3,2,1,0:T(8,128)} %bitcast.1, ...), custom_call_target="tpu_custom_call" | custom-call | tf_op jit(solution)/shard_map/outgoing/pallas_call | solution.py:201
  1.3 0.7 %collective-permute-start = (f32[2,128,128]{2,1,0:T(8,128)S(1)}, f32[2,128,128]{2,1,0:T(8,128)S(1)}, u32[]{:S(2)}, u32[]{:S(2)}) collective-permute-start(f32[2,128,128]{2,1,0:T(8,128)S(1)} %get-tuple-element.16.rest_0_), channel_id=1, source_target_pairs={{0,16},{1,17},{2,18},{3,19},{4,20},{5,21},{6,22},{7,23},{8,24},{9,... | collective-permute-start | bytes 393224 | tf_op jit(solution)/shard_map/ppermute | solution.py:217
  1.9 6.0 %collective-permute-start.1 = (f32[2,128,128]{2,1,0:T(8,128)S(1)}, f32[2,128,128]{2,1,0:T(8,128)S(1)}, u32[]{:S(2)}, u32[]{:S(2)}) collective-permute-start(f32[2,128,128]{2,1,0:T(8,128)S(1)} %get-tuple-element.17.rest_1_), channel_id=1, source_target_pairs={{3,4},{4,3},{7,8},{8,7},{11,12},{12,11},{16,32},{17,33},{18,34},{1... | collective-permute-start | bytes 393224 | tf_op jit(solution)/shard_map/ppermute | solution.py:217
  8.0 1.9 %collective-permute-start.2 = (f32[2,128,128]{2,1,0:T(8,128)S(1)}, f32[2,128,128]{2,1,0:T(8,128)S(1)}, u32[]{:S(2)}, u32[]{:S(2)}) collective-permute-start(f32[2,128,128]{2,1,0:T(8,128)S(1)} %get-tuple-element.18.rest_2_.rest_0_), channel_id=1, source_target_pairs={{0,1},{1,0},{2,3},{3,2},{4,5},{5,4},{6,7},{7,6},{8,9},{9,8},{10,11... | collective-permute-start | bytes 393224 | tf_op jit(solution)/shard_map/ppermute | solution.py:217
  9.9 0.7 %collective-permute-start.3 = (f32[2,128,128]{2,1,0:T(8,128)S(1)}, f32[2,128,128]{2,1,0:T(8,128)S(1)}, u32[]{:S(2)}, u32[]{:S(2)}) collective-permute-start(f32[2,128,128]{2,1,0:T(8,128)S(1)} %get-tuple-element.19.rest_3_.rest_1_), channel_id=1, source_target_pairs={{1,2},{2,1},{5,6},{6,5},{9,10},{10,9},{13,14},{14,13},{16,17},{17,... | collective-permute-start | bytes 393224 | tf_op jit(solution)/shard_map/ppermute | solution.py:217
  10.6 0.7 %collective-permute-start.4 = (f32[2,128,128]{2,1,0:T(8,128)S(1)}, f32[2,128,128]{2,1,0:T(8,128)S(1)}, u32[]{:S(2)}, u32[]{:S(2)}) collective-permute-start(f32[2,128,128]{2,1,0:T(8,128)S(1)} %get-tuple-element.20.rest_4_.rest_2_), channel_id=1, source_target_pairs={{0,64},{1,65},{2,66},{3,67},{4,68},{5,69},{6,70},{7,71},{8,72},{9,... | collective-permute-start | bytes 393224 | tf_op jit(solution)/shard_map/ppermute | solution.py:217
  11.2 0.0 collective-permute-done.rest_7_
  11.3 3.2 %collective-permute-start.5 = (f32[2,128,128]{2,1,0:T(8,128)S(1)}, f32[2,128,128]{2,1,0:T(8,128)S(1)}, u32[]{:S(2)}, u32[]{:S(2)}) collective-permute-start(f32[2,128,128]{2,1,0:T(8,128)S(1)} %get-tuple-element.21.rest_5_.rest_3_), channel_id=1, source_target_pairs={{16,80},{17,81},{18,82},{19,83},{20,84},{21,85},{22,86},{23,87},{2... | collective-permute-start | bytes 393224 | tf_op jit(solution)/shard_map/ppermute | solution.py:217
  14.4 6.9 %collective-permute-done.1.rest_8_ = f32[2,128,128]{2,1,0:T(8,128)S(1)} collective-permute-done((f32[2,128,128]{2,1,0:T(8,128)S(1)}, f32[2,128,128]{2,1,0:T(8,128)S(1)}, u32[]{:S(2)}, u32[]{:S(2)}) %collective-permute-start.1) | collective-permute-done | bytes 131104 | tf_op jit(solution)/shard_map/ppermute | solution.py:217
  21.3 1.9 %collective-permute-start.6 = (f32[2,128,128]{2,1,0:T(8,128)S(1)}, f32[2,128,128]{2,1,0:T(8,128)S(1)}, u32[]{:S(2)}, u32[]{:S(2)}) collective-permute-start(f32[2,128,128]{2,1,0:T(8,128)S(1)} %get-tuple-element.22.rest_6_.rest_4_), channel_id=1, source_target_pairs={{32,96},{33,97},{34,98},{35,99},{36,100},{37,101},{38,102},{39,103... | collective-permute-start | bytes 393224 | tf_op jit(solution)/shard_map/ppermute | solution.py:217
  23.2 0.6 %early.1 = (f32[9,128,128]{2,1,0:T(8,128)S(1)}, bf16[384,1024]{1,0:T(8,128)(2,1)S(1)}) custom-call(f32[7,8,128]{2,1,0:T(8,128)S(1)} %get-tuple-element.15.uses, f32[2,128,128]{2,1,0:T(8,128)S(1)} %get-tuple-element.16.rest_0_, f32[2,128,128]{2,1,0:T(8,128)S(1)} %get-tuple-element.17.rest_1_, f32[2,128,128]{2,1,0:T(8,128)S(1)} %get-tuple-element.18.rest_2_.rest_0_, ...), custom_call_target="tpu_custom_call" | custom-call | tf_op jit(solution)/shard_map/early/pallas_call | solution.py:220
  23.9 3.3 %collective-permute-done.2.rest_5_ = f32[2,128,128]{2,1,0:T(8,128)S(1)} collective-permute-done((f32[2,128,128]{2,1,0:T(8,128)S(1)}, f32[2,128,128]{2,1,0:T(8,128)S(1)}, u32[]{:S(2)}, u32[]{:S(2)}) %collective-permute-start.2) | collective-permute-done | bytes 131104 | tf_op jit(solution)/shard_map/ppermute | solution.py:217
  27.2 0.0 collective-permute-done.3.rest_6_
  27.2 0.0 collective-permute-done.4.rest_7_
  27.2 0.0 collective-permute-done.5.rest_8_
  27.2 0.0 collective-permute-done.6.rest_9_
  27.2 1.7 %finish.1 = f32[1,1,1,8,128,128]{5,4,3,2,1,0:T(8,128)} custom-call(f32[7,8,128]{2,1,0:T(8,128)S(1)} %get-tuple-element.15.uses, f32[9,128,128]{2,1,0:T(8,128)S(1)} %get-tuple-element.23.partial, bf16[384,1024]{1,0:T(8,128)(2,1)S(1)} %get-tuple-element.24.row_in, f32[2,128,128]{2,1,0:T(8,128)S(1)} %get-tuple-element.18.rest_2_.rest_0_, ...), custom_call_target="tpu_custom_call" | custom-call | tf_op jit(solution)/shard_map/finish/pallas_call | solution.py:231
Async XLA Ops:
  1.3 10.0 %collective-permute-start = (f32[2,128,128]{2,1,0:T(8,128)S(1)}, f32[2,128,128]{2,1,0:T(8,128)S(1)}, u32[]{:S(2)}, u32[]{:S(2)}) collective-permute-start(f32[2,128,128]{2,1,0:T(8,128)S(1)} %get-tuple-element.16.rest_0_), channel_id=1, source_target_pairs={{0,16},{1,17},{2,18},{3,19},{4,20},{5,21},{6,22},{7,23},{8,24},{9,... | collective-permute-start | bytes 393224 | tf_op jit(solution)/shard_map/ppermute | solution.py:217
  1.9 19.4 %collective-permute-start.1 = (f32[2,128,128]{2,1,0:T(8,128)S(1)}, f32[2,128,128]{2,1,0:T(8,128)S(1)}, u32[]{:S(2)}, u32[]{:S(2)}) collective-permute-start(f32[2,128,128]{2,1,0:T(8,128)S(1)} %get-tuple-element.17.rest_1_), channel_id=1, source_target_pairs={{3,4},{4,3},{7,8},{8,7},{11,12},{12,11},{16,32},{17,33},{18,34},{1... | collective-permute-start | bytes 393224 | tf_op jit(solution)/shard_map/ppermute | solution.py:217
  8.0 19.2 %collective-permute-start.2 = (f32[2,128,128]{2,1,0:T(8,128)S(1)}, f32[2,128,128]{2,1,0:T(8,128)S(1)}, u32[]{:S(2)}, u32[]{:S(2)}) collective-permute-start(f32[2,128,128]{2,1,0:T(8,128)S(1)} %get-tuple-element.18.rest_2_.rest_0_), channel_id=1, source_target_pairs={{0,1},{1,0},{2,3},{3,2},{4,5},{5,4},{6,7},{7,6},{8,9},{9,8},{10,11... | collective-permute-start | bytes 393224 | tf_op jit(solution)/shard_map/ppermute | solution.py:217
  9.9 17.3 %collective-permute-start.3 = (f32[2,128,128]{2,1,0:T(8,128)S(1)}, f32[2,128,128]{2,1,0:T(8,128)S(1)}, u32[]{:S(2)}, u32[]{:S(2)}) collective-permute-start(f32[2,128,128]{2,1,0:T(8,128)S(1)} %get-tuple-element.19.rest_3_.rest_1_), channel_id=1, source_target_pairs={{1,2},{2,1},{5,6},{6,5},{9,10},{10,9},{13,14},{14,13},{16,17},{17,... | collective-permute-start | bytes 393224 | tf_op jit(solution)/shard_map/ppermute | solution.py:217
  10.6 16.6 %collective-permute-start.4 = (f32[2,128,128]{2,1,0:T(8,128)S(1)}, f32[2,128,128]{2,1,0:T(8,128)S(1)}, u32[]{:S(2)}, u32[]{:S(2)}) collective-permute-start(f32[2,128,128]{2,1,0:T(8,128)S(1)} %get-tuple-element.20.rest_4_.rest_2_), channel_id=1, source_target_pairs={{0,64},{1,65},{2,66},{3,67},{4,68},{5,69},{6,70},{7,71},{8,72},{9,... | collective-permute-start | bytes 393224 | tf_op jit(solution)/shard_map/ppermute | solution.py:217
  11.3 15.9 %collective-permute-start.5 = (f32[2,128,128]{2,1,0:T(8,128)S(1)}, f32[2,128,128]{2,1,0:T(8,128)S(1)}, u32[]{:S(2)}, u32[]{:S(2)}) collective-permute-start(f32[2,128,128]{2,1,0:T(8,128)S(1)} %get-tuple-element.21.rest_5_.rest_3_), channel_id=1, source_target_pairs={{16,80},{17,81},{18,82},{19,83},{20,84},{21,85},{22,86},{23,87},{2... | collective-permute-start | bytes 393224 | tf_op jit(solution)/shard_map/ppermute | solution.py:217
  21.3 5.9 %collective-permute-start.6 = (f32[2,128,128]{2,1,0:T(8,128)S(1)}, f32[2,128,128]{2,1,0:T(8,128)S(1)}, u32[]{:S(2)}, u32[]{:S(2)}) collective-permute-start(f32[2,128,128]{2,1,0:T(8,128)S(1)} %get-tuple-element.22.rest_6_.rest_4_), channel_id=1, source_target_pairs={{32,96},{33,97},{34,98},{35,99},{36,100},{37,101},{38,102},{39,103... | collective-permute-start | bytes 393224 | tf_op jit(solution)/shard_map/ppermute | solution.py:217

commit v7 on v6

--- a/solution.py
+++ b/solution.py
@@ -193,7 +193,7 @@
     partners = pltpu.with_memory_space_constraint(partners, pltpu.HBM)
     blocks = pltpu.with_memory_space_constraint(blocks, pltpu.HBM)
     count = len(ROUNDS)
-    parts = 4
+    parts = 2
     vmem = pl.BlockSpec(memory_space=pltpu.VMEM)
     hbm = pl.BlockSpec(memory_space=pltpu.HBM)
     params = pltpu.CompilerParams(vmem_limit_bytes=VMEM_BYTES)

time: 29.2 us -> 29.1 us (level)
  no operation moved by 1% of the time
where the time goes in v7:
time: 29.1 us; the launch traced here: 28.9 us
  starting transfers between devices  15 us (52%)
  waiting for transfers between devices  10.2 us (35%)
  Pallas kernels  3.55 us (12%)
    ppermute x7, starting transfers between devices, on_device(): lax.ppermute(send, AXES, [(i, int(j)) for i, j in enumerate(row.ravel())...  15 us
    ppermute x7, waiting for transfers between devices, on_device(): lax.ppermute(send, AXES, [(i, int(j)) for i, j in enumerate(row.ravel())...  10.2 us
    pallas_call x1, Pallas kernels, on_device(): pl.pallas_call(finish, out_shape=jax.ShapeDtypeStruct(blocks.shape, jnp.f...  1.71 us
    pallas_call x1, Pallas kernels, on_device(): pl.pallas_call(functools.partial(outgoing, parts), out_shape=(pair,) * co...  1.23 us
    pallas_call x1, Pallas kernels, on_device(): pl.pallas_call(early, out_shape=(jax.ShapeDtypeStruct((count + 2, size, s...  0.62 us
  transfers between devices with their start and end apart: 7, of which 2 were waited for; matrix products, arithmetic and copies ran while one was open for 0% of the time, Pallas kernels for 2%

profile of v7, /device:TPU:256, one launch (start us, length us, event | category | flops | bytes accessed | tf_op | source)
XLA Modules:
  0.0 28.9 jit_solution(10015679890531415766)
XLA Ops:
  0.0 1.2 %outgoing.1 = (f32[2,128,128]{2,1,0:T(8,128)S(1)}, f32[2,128,128]{2,1,0:T(8,128)S(1)}, f32[2,128,128]{2,1,0:T(8,128)S(1)}, f32[2,128,128]{2,1,0:T(8,128)S(1)}, f...) custom-call(s32[8,4,8,16]{3,2,1,0:T(8,128)} %bitcast.1, ...), custom_call_target="tpu_custom_call" | custom-call | tf_op jit(solution)/shard_map/outgoing/pallas_call | solution.py:201
  1.2 0.7 %collective-permute-start = (f32[2,128,128]{2,1,0:T(8,128)S(1)}, f32[2,128,128]{2,1,0:T(8,128)S(1)}, u32[]{:S(2)}, u32[]{:S(2)}) collective-permute-start(f32[2,128,128]{2,1,0:T(8,128)S(1)} %get-tuple-element.16.rest_0_), channel_id=1, source_target_pairs={{0,16},{1,17},{2,18},{3,19},{4,20},{5,21},{6,22},{7,23},{8,24},{9,... | collective-permute-start | bytes 393224 | tf_op jit(solution)/shard_map/ppermute | solution.py:217
  1.9 6.0 %collective-permute-start.1 = (f32[2,128,128]{2,1,0:T(8,128)S(1)}, f32[2,128,128]{2,1,0:T(8,128)S(1)}, u32[]{:S(2)}, u32[]{:S(2)}) collective-permute-start(f32[2,128,128]{2,1,0:T(8,128)S(1)} %get-tuple-element.17.rest_1_), channel_id=1, source_target_pairs={{3,4},{4,3},{7,8},{8,7},{11,12},{12,11},{16,32},{17,33},{18,34},{1... | collective-permute-start | bytes 393224 | tf_op jit(solution)/shard_map/ppermute | solution.py:217
  7.9 1.9 %collective-permute-start.2 = (f32[2,128,128]{2,1,0:T(8,128)S(1)}, f32[2,128,128]{2,1,0:T(8,128)S(1)}, u32[]{:S(2)}, u32[]{:S(2)}) collective-permute-start(f32[2,128,128]{2,1,0:T(8,128)S(1)} %get-tuple-element.18.rest_2_.rest_0_), channel_id=1, source_target_pairs={{0,1},{1,0},{2,3},{3,2},{4,5},{5,4},{6,7},{7,6},{8,9},{9,8},{10,11... | collective-permute-start | bytes 393224 | tf_op jit(solution)/shard_map/ppermute | solution.py:217
  9.9 0.7 %collective-permute-start.3 = (f32[2,128,128]{2,1,0:T(8,128)S(1)}, f32[2,128,128]{2,1,0:T(8,128)S(1)}, u32[]{:S(2)}, u32[]{:S(2)}) collective-permute-start(f32[2,128,128]{2,1,0:T(8,128)S(1)} %get-tuple-element.19.rest_3_.rest_1_), channel_id=1, source_target_pairs={{1,2},{2,1},{5,6},{6,5},{9,10},{10,9},{13,14},{14,13},{16,17},{17,... | collective-permute-start | bytes 393224 | tf_op jit(solution)/shard_map/ppermute | solution.py:217
  10.5 0.7 %collective-permute-start.4 = (f32[2,128,128]{2,1,0:T(8,128)S(1)}, f32[2,128,128]{2,1,0:T(8,128)S(1)}, u32[]{:S(2)}, u32[]{:S(2)}) collective-permute-start(f32[2,128,128]{2,1,0:T(8,128)S(1)} %get-tuple-element.20.rest_4_.rest_2_), channel_id=1, source_target_pairs={{0,64},{1,65},{2,66},{3,67},{4,68},{5,69},{6,70},{7,71},{8,72},{9,... | collective-permute-start | bytes 393224 | tf_op jit(solution)/shard_map/ppermute | solution.py:217
  11.2 0.0 collective-permute-done.rest_7_
  11.2 3.2 %collective-permute-start.5 = (f32[2,128,128]{2,1,0:T(8,128)S(1)}, f32[2,128,128]{2,1,0:T(8,128)S(1)}, u32[]{:S(2)}, u32[]{:S(2)}) collective-permute-start(f32[2,128,128]{2,1,0:T(8,128)S(1)} %get-tuple-element.21.rest_5_.rest_3_), channel_id=1, source_target_pairs={{16,80},{17,81},{18,82},{19,83},{20,84},{21,85},{22,86},{23,87},{2... | collective-permute-start | bytes 393224 | tf_op jit(solution)/shard_map/ppermute | solution.py:217
  14.4 6.9 %collective-permute-done.1.rest_8_ = f32[2,128,128]{2,1,0:T(8,128)S(1)} collective-permute-done((f32[2,128,128]{2,1,0:T(8,128)S(1)}, f32[2,128,128]{2,1,0:T(8,128)S(1)}, u32[]{:S(2)}, u32[]{:S(2)}) %collective-permute-start.1) | collective-permute-done | bytes 131104 | tf_op jit(solution)/shard_map/ppermute | solution.py:217
  21.3 1.9 %collective-permute-start.6 = (f32[2,128,128]{2,1,0:T(8,128)S(1)}, f32[2,128,128]{2,1,0:T(8,128)S(1)}, u32[]{:S(2)}, u32[]{:S(2)}) collective-permute-start(f32[2,128,128]{2,1,0:T(8,128)S(1)} %get-tuple-element.22.rest_6_.rest_4_), channel_id=1, source_target_pairs={{32,96},{33,97},{34,98},{35,99},{36,100},{37,101},{38,102},{39,103... | collective-permute-start | bytes 393224 | tf_op jit(solution)/shard_map/ppermute | solution.py:217
  23.2 0.6 %early.1 = (f32[9,128,128]{2,1,0:T(8,128)S(1)}, bf16[384,1024]{1,0:T(8,128)(2,1)S(1)}) custom-call(f32[7,8,128]{2,1,0:T(8,128)S(1)} %get-tuple-element.15.uses, f32[2,128,128]{2,1,0:T(8,128)S(1)} %get-tuple-element.16.rest_0_, f32[2,128,128]{2,1,0:T(8,128)S(1)} %get-tuple-element.17.rest_1_, f32[2,128,128]{2,1,0:T(8,128)S(1)} %get-tuple-element.18.rest_2_.rest_0_, ...), custom_call_target="tpu_custom_call" | custom-call | tf_op jit(solution)/shard_map/early/pallas_call | solution.py:220
  23.8 3.3 %collective-permute-done.2.rest_5_ = f32[2,128,128]{2,1,0:T(8,128)S(1)} collective-permute-done((f32[2,128,128]{2,1,0:T(8,128)S(1)}, f32[2,128,128]{2,1,0:T(8,128)S(1)}, u32[]{:S(2)}, u32[]{:S(2)}) %collective-permute-start.2) | collective-permute-done | bytes 131104 | tf_op jit(solution)/shard_map/ppermute | solution.py:217
  27.1 0.0 collective-permute-done.3.rest_6_
  27.1 0.0 collective-permute-done.4.rest_7_
  27.1 0.0 collective-permute-done.5.rest_8_
  27.1 0.0 collective-permute-done.6.rest_9_
  27.1 1.7 %finish.1 = f32[1,1,1,8,128,128]{5,4,3,2,1,0:T(8,128)} custom-call(f32[7,8,128]{2,1,0:T(8,128)S(1)} %get-tuple-element.15.uses, f32[9,128,128]{2,1,0:T(8,128)S(1)} %get-tuple-element.23.partial, bf16[384,1024]{1,0:T(8,128)(2,1)S(1)} %get-tuple-element.24.row_in, f32[2,128,128]{2,1,0:T(8,128)S(1)} %get-tuple-element.18.rest_2_.rest_0_, ...), custom_call_target="tpu_custom_call" | custom-call | tf_op jit(solution)/shard_map/finish/pallas_call | solution.py:231
Async XLA Ops:
  1.2 10.0 %collective-permute-start = (f32[2,128,128]{2,1,0:T(8,128)S(1)}, f32[2,128,128]{2,1,0:T(8,128)S(1)}, u32[]{:S(2)}, u32[]{:S(2)}) collective-permute-start(f32[2,128,128]{2,1,0:T(8,128)S(1)} %get-tuple-element.16.rest_0_), channel_id=1, source_target_pairs={{0,16},{1,17},{2,18},{3,19},{4,20},{5,21},{6,22},{7,23},{8,24},{9,... | collective-permute-start | bytes 393224 | tf_op jit(solution)/shard_map/ppermute | solution.py:217
  1.9 19.4 %collective-permute-start.1 = (f32[2,128,128]{2,1,0:T(8,128)S(1)}, f32[2,128,128]{2,1,0:T(8,128)S(1)}, u32[]{:S(2)}, u32[]{:S(2)}) collective-permute-start(f32[2,128,128]{2,1,0:T(8,128)S(1)} %get-tuple-element.17.rest_1_), channel_id=1, source_target_pairs={{3,4},{4,3},{7,8},{8,7},{11,12},{12,11},{16,32},{17,33},{18,34},{1... | collective-permute-start | bytes 393224 | tf_op jit(solution)/shard_map/ppermute | solution.py:217
  7.9 19.2 %collective-permute-start.2 = (f32[2,128,128]{2,1,0:T(8,128)S(1)}, f32[2,128,128]{2,1,0:T(8,128)S(1)}, u32[]{:S(2)}, u32[]{:S(2)}) collective-permute-start(f32[2,128,128]{2,1,0:T(8,128)S(1)} %get-tuple-element.18.rest_2_.rest_0_), channel_id=1, source_target_pairs={{0,1},{1,0},{2,3},{3,2},{4,5},{5,4},{6,7},{7,6},{8,9},{9,8},{10,11... | collective-permute-start | bytes 393224 | tf_op jit(solution)/shard_map/ppermute | solution.py:217
  9.9 17.3 %collective-permute-start.3 = (f32[2,128,128]{2,1,0:T(8,128)S(1)}, f32[2,128,128]{2,1,0:T(8,128)S(1)}, u32[]{:S(2)}, u32[]{:S(2)}) collective-permute-start(f32[2,128,128]{2,1,0:T(8,128)S(1)} %get-tuple-element.19.rest_3_.rest_1_), channel_id=1, source_target_pairs={{1,2},{2,1},{5,6},{6,5},{9,10},{10,9},{13,14},{14,13},{16,17},{17,... | collective-permute-start | bytes 393224 | tf_op jit(solution)/shard_map/ppermute | solution.py:217
  10.5 16.6 %collective-permute-start.4 = (f32[2,128,128]{2,1,0:T(8,128)S(1)}, f32[2,128,128]{2,1,0:T(8,128)S(1)}, u32[]{:S(2)}, u32[]{:S(2)}) collective-permute-start(f32[2,128,128]{2,1,0:T(8,128)S(1)} %get-tuple-element.20.rest_4_.rest_2_), channel_id=1, source_target_pairs={{0,64},{1,65},{2,66},{3,67},{4,68},{5,69},{6,70},{7,71},{8,72},{9,... | collective-permute-start | bytes 393224 | tf_op jit(solution)/shard_map/ppermute | solution.py:217
  11.2 15.9 %collective-permute-start.5 = (f32[2,128,128]{2,1,0:T(8,128)S(1)}, f32[2,128,128]{2,1,0:T(8,128)S(1)}, u32[]{:S(2)}, u32[]{:S(2)}) collective-permute-start(f32[2,128,128]{2,1,0:T(8,128)S(1)} %get-tuple-element.21.rest_5_.rest_3_), channel_id=1, source_target_pairs={{16,80},{17,81},{18,82},{19,83},{20,84},{21,85},{22,86},{23,87},{2... | collective-permute-start | bytes 393224 | tf_op jit(solution)/shard_map/ppermute | solution.py:217
  21.3 5.9 %collective-permute-start.6 = (f32[2,128,128]{2,1,0:T(8,128)S(1)}, f32[2,128,128]{2,1,0:T(8,128)S(1)}, u32[]{:S(2)}, u32[]{:S(2)}) collective-permute-start(f32[2,128,128]{2,1,0:T(8,128)S(1)} %get-tuple-element.22.rest_6_.rest_4_), channel_id=1, source_target_pairs={{32,96},{33,97},{34,98},{35,99},{36,100},{37,101},{38,102},{39,103... | collective-permute-start | bytes 393224 | tf_op jit(solution)/shard_map/ppermute | solution.py:217
